TPU v7x, 32 devices: a whole 2x2x4 slice. The times are simulated.
32 devices in a mesh: tu: 8 (over z, x), tv: 4 (over y, core).
Axes of the slice: x: 2, y: 2, z: 4, core: 2. Of those that a mesh axis runs over, the one named last changes fastest.
Arguments:
- aperture_amp: bfloat16 [128, 512, 512], P(('tu', 'tv')), may hold values from 0.19921875 to 1.796875
- aperture_phase: bfloat16 [128, 512, 512], P(('tu', 'tv')), may hold values from -3.140625 to 3.140625
- plane_depths: float32 [4], replicated, may hold values from 8 to 344
- send_list: int32 [32, 32, 2], P(('tu', 'tv')), may hold values from 0 to 15, as said below
- send_count: int32 [32, 32], P(('tu', 'tv')), may hold values from 0 to 2, as said below
- vis_left: bfloat16 [12288, 128, 128], P(('tu', 'tv')), may hold values from -0.078125 to 0.078125
- vis_right: bfloat16 [12288, 64, 128], P(('tu', 'tv')), may hold values from -0.75 to 0.75
- block_slot: int32 [12288], P(('tu', 'tv')), may hold values from 0 to 63, as said below
- block_pos: int32 [12288], P(('tu', 'tv')), may hold values from 0 to 31
- block_count: int32 [32], P(('tu', 'tv')), may hold values from 96 to 384, as said below
Outputs:
- uv_grid: float32 [2, 2048, 2048], P(None, 'tu', 'tv')
Inputs may be any that keep to these rules, and one draw needn't show every extreme that they name: `send_list`: each owner sends every one of its kernels to 2 slots, 32 in all; the used slots of an owner and tile are the first send_count of them; entries of unused slots are arbitrary kernel numbers in range. One tile, drawn afresh, receives 2 slots from every owner; a row of send_count sums to 32. `block_slot`: names a slot r = d * 2 + c that the block's tile receives, with c < send_count[d, tile]. `block_count`: some tile uses all 384 slots.
All inputs are finite; a program needn't handle non-finite values.
Results may differ from a plain program's by a relative error of at most 0.0065.
Values may be sent and summed in bfloat16 or wider, within the bound.
No kernel may reach another device: no remote copies, remote signals or barrier semaphores. Data moves between devices by JAX's collectives and lax.ppermute only.
A program may use at most 192 MiB of HBM per device.

v0:
```python
import math

import jax
import jax.numpy as jnp
from jax import lax
from jax.sharding import PartitionSpec as P

KSIZE = 64
TILE_U = 256
TILE_V = 512


def from_behind(block, axis, distance):
    devices = range(lax.axis_size(axis))
    route = [(i - distance, i) for i in devices if i - distance in devices]
    return lax.ppermute(block, axis, route)


def dft_table(kernel_size, screen_size):
    frequency = jnp.arange(kernel_size, dtype=jnp.int32) - kernel_size // 2
    cell_ids = jnp.arange(screen_size, dtype=jnp.int32)
    turns = jnp.mod(frequency[:, None] * cell_ids[None, :], screen_size).astype(jnp.float32)
    angles = 2.0 * math.pi / screen_size * turns
    return jnp.concatenate([jnp.cos(angles), -jnp.sin(angles)], axis=0).astype(jnp.bfloat16)


def aperture_screens(amplitude, phase_rows, plane_depths):
    screen_size = amplitude.shape[-1]
    coords = (
        jnp.arange(screen_size, dtype=jnp.int32).astype(jnp.float32) - screen_size // 2
    ) / screen_size
    radius = coords[:, None] ** 2 + coords[None, :] ** 2
    angles = (
        phase_rows.astype(jnp.float32)[:, None]
        + 2.0 * math.pi * plane_depths[None, :, None, None] * radius
    )
    magnitude = amplitude.astype(jnp.float32)[:, None]
    real_part = (magnitude * jnp.cos(angles)).astype(jnp.bfloat16)
    imag_part = (magnitude * jnp.sin(angles)).astype(jnp.bfloat16)
    stacked = jnp.concatenate([real_part, imag_part], axis=-1)
    return stacked.reshape(-1, screen_size, 2 * screen_size)


def kernels_from(stacked, kernel_size):
    screen_size = stacked.shape[1]
    dft = dft_table(kernel_size, screen_size)
    product = jnp.einsum("as,ksn->kan", dft, stacked, preferred_element_type=jnp.float32)
    half_real = product[:, :kernel_size, :screen_size] - product[:, kernel_size:, screen_size:]
    half_imag = product[:, :kernel_size, screen_size:] + product[:, kernel_size:, :screen_size]
    halves = jnp.concatenate([half_real, half_imag], axis=1).astype(jnp.bfloat16)
    second = jnp.einsum("kas,bs->kab", halves, dft, preferred_element_type=jnp.float32)
    out_real = second[:, :kernel_size, :kernel_size] - second[:, kernel_size:, kernel_size:]
    out_imag = second[:, :kernel_size, kernel_size:] + second[:, kernel_size:, :kernel_size]
    return (jnp.concatenate([out_real, out_imag], axis=-1) / screen_size).astype(jnp.bfloat16)


def grid_patches(block_kernels, left_rows, right_rows):
    kernel_size = block_kernels.shape[1]
    real_k = block_kernels[:, :, :kernel_size]
    imag_k = block_kernels[:, :, kernel_size:]
    operator_rows = jnp.concatenate(
        [block_kernels, jnp.concatenate([-imag_k, real_k], axis=2)], axis=1
    )
    mixed = jnp.einsum(
        "gpc,gcd->gpd", left_rows, operator_rows, preferred_element_type=jnp.float32
    ).astype(jnp.bfloat16)
    stacked_rows = mixed.reshape(mixed.shape[0], 2 * mixed.shape[1], kernel_size)
    return jnp.einsum("grk,gkq->grq", stacked_rows, right_rows, preferred_element_type=jnp.float32)


def split_groups(values, group_count):
    return values.reshape((group_count, values.shape[0] // group_count) + values.shape[1:])


def shards(
    aperture_amp,
    aperture_phase,
    plane_depths,
    send_list,
    send_count,
    vis_left,
    vis_right,
    block_slot,
    block_pos,
    block_count,
):
    kernels = kernels_from(aperture_screens(aperture_amp, aperture_phase, plane_depths), KSIZE)
    send_rows = send_list[0]
    counts = send_count[0]
    capacity = send_rows.shape[1]
    is_live = jnp.arange(capacity, dtype=jnp.int32)[None, :] < counts[:, None]
    outgoing = jnp.where(is_live[:, :, None, None], kernels[send_rows], jnp.zeros((), jnp.bfloat16))
    arrived = lax.all_to_all(outgoing, ("tu", "tv"), split_axis=0, concat_axis=0, tiled=True)
    received = arrived.reshape(-1, KSIZE, 2 * KSIZE)
    block_total = vis_left.shape[0]
    group_size = min(128, block_total)
    group_count = block_total // group_size
    row_slots = TILE_U // KSIZE
    col_slots = TILE_V // KSIZE
    ext_cols = col_slots + 1
    ext_total = (row_slots + 1) * ext_cols
    block_ids = jnp.arange(block_total, dtype=jnp.int32)
    targets = jnp.arange(ext_total, dtype=jnp.int32)
    tile_count = block_count[0]

    def grid_group(placed, grouped):
        left_rows, right_rows, slot_ids, positions, member_ids = grouped
        patches = grid_patches(received[slot_ids], left_rows, right_rows)
        quarters = patches.reshape(group_size, 2, KSIZE, 2, 2, KSIZE)
        row_anchor = positions // col_slots
        col_anchor = positions % col_slots
        member_live = member_ids < tile_count
        for row_half in range(2):
            for col_half in range(2):
                dest = (row_anchor + row_half) * ext_cols + col_anchor + col_half
                onehot = ((dest[None, :] == targets[:, None]) & member_live[None, :]).astype(
                    jnp.float32
                )
                piece = quarters[:, row_half, :, :, col_half, :].reshape(group_size, -1)
                placed = placed + jnp.dot(onehot, piece, precision=lax.Precision.HIGHEST)
        return (placed, None)

    grouped = (
        split_groups(vis_left, group_count),
        split_groups(vis_right, group_count),
        split_groups(block_slot, group_count),
        split_groups(block_pos, group_count),
        split_groups(block_ids, group_count),
    )
    start = jnp.zeros((ext_total, 2 * KSIZE * KSIZE), jnp.float32)
    placed, unused = lax.scan(grid_group, start, grouped)
    extended = placed.reshape(row_slots + 1, ext_cols, KSIZE, 2, KSIZE).transpose(3, 0, 2, 1, 4)
    extended = extended.reshape(2, (row_slots + 1) * KSIZE, ext_cols * KSIZE)
    bottom = extended[:, TILE_U:, :]
    arrived_rows = from_behind(bottom.astype(jnp.bfloat16), "tu", 1).astype(bottom.dtype)
    extended = extended.at[:, :KSIZE, :].add(arrived_rows)
    side = extended[:, :TILE_U, TILE_V:]
    arrived_cols = from_behind(side.astype(jnp.bfloat16), "tv", 1).astype(side.dtype)
    result = extended[:, :TILE_U, :TILE_V].at[:, :, :KSIZE].add(arrived_cols)
    return result


def solution(mesh):
    placed = (
        P(("tu", "tv"), None, None),
        P(("tu", "tv"), None, None),
        P(),
        P(("tu", "tv"), None, None),
        P(("tu", "tv"), None),
        P(("tu", "tv"), None, None),
        P(("tu", "tv"), None, None),
        P(("tu", "tv")),
        P(("tu", "tv")),
        P(("tu", "tv")),
    )
    return jax.shard_map(
        shards, mesh=mesh, in_specs=placed, out_specs=P(None, "tu", "tv"), check_vma=False
    )
```

profile of v0, /device:TPU:0, one launch (start us, length us, event | category | flops | bytes accessed | tf_op | source)
XLA Modules:
  0.0 383.3 jit_solution(14202420143690126748)
XLA Ops:
  0.8 0.7 broadcast_multiply_fusion.1
  1.4 2.2 convert_element_type.59
  4.2 0.7 broadcast_multiply_fusion
  4.9 61.6 %fusion.42 = (bf16[4,4,512,512]{3,2,1,0:T(8,128)(2,1)S(1)}, bf16[4,4,512,512]{3,2,1,0:T(8,128)(2,1)}) fusion(f32[4,512,512]{2,1,0:T(8,128)S(1)} %broadcast_multiply_fusion, f32[4,512,512]{2,1,0:T(8,128)S(1)} %convert_element_type.60, f32[4,512,512]{2,1,0:T(8,128)S(1)} %convert_element_type.59), kind=kLoop, calls=%fused_computation.61 | loop fusion | flops 20971520 | bytes 29360128 | tf_op jit(solution)/shard_map/convert_element_type | solution.py:38
  66.5 6.7 %fusion.49 = f32[16,128,1024]{2,1,0:T(8,128)} fusion(bf16[16,512,512]{2,1,0:T(8,128)(2,1)} %bitcast.106, bf16[16,512,512]{2,1,0:T(8,128)(2,1)S(1)} %bitcast.105, bf16[64,512]{1,0:T(8,128)(2,1)S(1)} %get-tuple-element.262, bf16[64,512]{1,0:T(8,128)(2,1)S(1)} %get-tuple-element.261), kind=kOutput, calls=%fused_computation.68 | convolution fusion | flops 2181300224 | bytes 25296896 | tf_op jit(solution)/shard_map/as,ksn->kan/dot_general | solution.py:47
  73.2 4.3 %fusion.53 = (bf16[16,64,512]{2,1,0:T(8,128)(2,1)S(1)}, bf16[16,64,512]{2,1,0:T(8,128)(2,1)S(1)}) fusion(f32[16,128,1024]{2,1,0:T(8,128)} %fusion.49), kind=kLoop, calls=%fused_computation.72 | loop fusion | flops 2097152 | bytes 10485760 | tf_op jit(solution)/shard_map/convert.2
  77.5 0.7 fusion.54
  79.1 0.7 gather_fusion.1
  79.8 1.1 broadcast_select_fusion
  80.9 7.3 %all-to-all-start = ((bf16[32,2,64,128]{3,2,1,0:T(8,128)(2,1)}), bf16[32,2,64,128]{3,2,1,0:T(8,128)(2,1)S(1)}, u32[]{:S(2)}, u32[]{:S(2)}) async-start(bf16[32,2,64,128]{3,2,1,0:T(8,128)(2,1)} %broadcast_select_fusion), calls=%async_computation | async-start | bytes 2097152 | tf_op jit(solution)/shard_map/all_to_all | solution.py:93
  88.3 26.2 %all-to-all-done = bf16[32,2,64,128]{3,2,1,0:T(8,128)(2,1)S(1)} async-done(((bf16[32,2,64,128]{3,2,1,0:T(8,128)(2,1)}), bf16[32,2,64,128]{3,2,1,0:T(8,128)(2,1)S(1)}, u32[]{:S(2)}, u32[]{:S(2)}) %all-to-all-start) | async-done | bytes 1048608 | tf_op jit(solution)/shard_map/all_to_all | solution.py:93
  114.5 236.6 %while.16 = (s32[]{:T(128)}, f32[45,8192]{1,0:T(8,128)}, s32[3,128]{1,0:T(4,128)}, s32[3,128]{1,0:T(4,128)S(1)}, s32[]{:T(128)}, /*index=5*/bf16[3,128,128,128]{...) while((s32[]{:T(128)}, f32[45,8192]{1,0:T(8,128)}, ...), condition=%wide.region_1.2_spmd.clone.clone, body=%wide.region_0.1_spmd.clone.clone.sunk | while | flops 3355764736 | bytes 212745104 | solution.py:131
  114.5 0.7 fusion.103
  115.2 0.9 gather_fusion
  116.1 0.9 slice_negate_fusion.2
  117.0 5.7 %fusion.104 = bf16[128,128,128]{2,1,0:T(8,128)(2,1)} fusion(bf16[128,64,64]{2,1,0:T(8,128)(2,1)S(1)} %get-tuple-element.330, bf16[128,64,64]{2,1,0:T(8,128)(2,1)S(1)} %get-tuple-element.331, bf16[128,64,128]{2,1,0:T(8,128)(2,1)S(1)} %gather_fusion, bf16[3,128,128,128]{3,2,1,0:T(8,128)(2,1)} %get-tuple-element.369, s32[]{:T(128)} %get-tuple-element.353), kind=kOutput, calls=%fused_computation.15.clone.1 | convolution fusion | flops 551550976 | bytes 12583424 | tf_op jit(solution)/shard_map/while/body/eval_jaxpr/gpc,gcd->gpd/dot_general | solution.py:64
  122.7 6.9 %copy.23 = bf16[128,128,128]{0,2,1:T(8,128)(2,1)} copy(bf16[128,128,128]{2,1,0:T(8,128)(2,1)} %fusion.104) | data formatting | bytes 8388608 | tf_op jit(solution)/shard_map/while/body/eval_jaxpr/convert_element_type | solution.py:66
  129.6 7.4 %copy.24 = bf16[128,256,64]{1,2,0:T(8,128)(2,1)} copy(bf16[128,256,64]{0,2,1:T(8,128)(2,1)} %bitcast.97) | data formatting | bytes 8388608 | tf_op jit(solution)/shard_map/while/body/eval_jaxpr/reshape | solution.py:67
  137.0 11.0 %fusion.105 = f32[128,256,128]{2,1,0:T(8,128)} fusion(bf16[128,256,64]{1,2,0:T(8,128)(2,1)} %copy.24, bf16[3,128,64,128]{3,2,1,0:T(8,128)(2,1)} %get-tuple-element.372, s32[]{:T(128)} %get-tuple-element.353), kind=kOutput, calls=%fused_computation.17.clone.1 | convolution fusion | flops 536870912 | bytes 23069184 | tf_op jit(solution)/shard_map/while/body/eval_jaxpr/grk,gkq->grq/dot_general | solution.py:68
  148.0 17.6 %copy.25 = f32[128,256,128]{0,2,1:T(8,128)} copy(f32[128,256,128]{2,1,0:T(8,128)} %fusion.105) | data formatting | bytes 33554432 | tf_op jit(solution)/shard_map/while/body/eval_jaxpr/grk,gkq->grq/dot_general | solution.py:68
  165.6 12.6 %fusion.106 = (f32[128,1,64,2,1,64]{0,5,4,3,2,1:T(8,128)}, f32[128,1,64,2,1,64]{0,5,4,3,2,1:T(8,128)}, f32[128,1,64,2,1,64]{0,5,4,3,2,1:T(8,128)}, f32[128,1,64,2,1,64]{0,5,4,3,2,1:T(8,128)}) fusion(f32[128,2,64,2,2,64]{0,5,4,3,2,1:T(8,128)} %bitcast.96), kind=kLoop, calls=%fused_computation.110.clone.1 | loop fusion | bytes 33554432 | tf_op jit(solution)/shard_map/while/body/eval_jaxpr/slice | solution.py:119
  178.1 0.7 add_bitcast_fusion.3
  178.9 0.7 compare_bitcast_fusion.2
  179.5 4.8 %convolution_add_fusion.8 = f32[45,8192]{1,0:T(8,128)S(1)} fusion(f32[128,8192]{0,1:T(8,128)} %bitcast.101, f32[45,8192]{1,0:T(8,128)S(1)} %copy-done.3, pred[]{:T(512)S(6)} %compare.37, s32[128]{0:T(128)S(1)} %get-tuple-element.335, pred[128]{0:T(512)(128)(4,1)S(1)} %compare_bitcast_fusion.2), kind=kOutput, calls=%fused_computation.6.clone.1 | convolution fusion | flops 566979840 | bytes 7144065 | tf_op jit(solution)/shard_map/while/body/eval_jaxpr/dot_general | solution.py:120
  184.4 2.6 convolution_add_fusion.9
  187.0 2.6 convolution_add_fusion.10
  189.6 3.7 convolution_add_fusion.11
  193.4 0.7 fusion.103
  194.1 0.9 gather_fusion
  195.0 0.9 slice_negate_fusion.2
  195.9 5.7 %fusion.104 = bf16[128,128,128]{2,1,0:T(8,128)(2,1)} fusion(bf16[128,64,64]{2,1,0:T(8,128)(2,1)S(1)} %get-tuple-element.330, bf16[128,64,64]{2,1,0:T(8,128)(2,1)S(1)} %get-tuple-element.331, bf16[128,64,128]{2,1,0:T(8,128)(2,1)S(1)} %gather_fusion, bf16[3,128,128,128]{3,2,1,0:T(8,128)(2,1)} %get-tuple-element.369, s32[]{:T(128)} %get-tuple-element.353), kind=kOutput, calls=%fused_computation.15.clone.1 | convolution fusion | flops 551550976 | bytes 12583424 | tf_op jit(solution)/shard_map/while/body/eval_jaxpr/gpc,gcd->gpd/dot_general | solution.py:64
  201.6 6.9 %copy.23 = bf16[128,128,128]{0,2,1:T(8,128)(2,1)} copy(bf16[128,128,128]{2,1,0:T(8,128)(2,1)} %fusion.104) | data formatting | bytes 8388608 | tf_op jit(solution)/shard_map/while/body/eval_jaxpr/convert_element_type | solution.py:66
  208.5 7.4 %copy.24 = bf16[128,256,64]{1,2,0:T(8,128)(2,1)} copy(bf16[128,256,64]{0,2,1:T(8,128)(2,1)} %bitcast.97) | data formatting | bytes 8388608 | tf_op jit(solution)/shard_map/while/body/eval_jaxpr/reshape | solution.py:67
  215.9 11.0 %fusion.105 = f32[128,256,128]{2,1,0:T(8,128)} fusion(bf16[128,256,64]{1,2,0:T(8,128)(2,1)} %copy.24, bf16[3,128,64,128]{3,2,1,0:T(8,128)(2,1)} %get-tuple-element.372, s32[]{:T(128)} %get-tuple-element.353), kind=kOutput, calls=%fused_computation.17.clone.1 | convolution fusion | flops 536870912 | bytes 23069184 | tf_op jit(solution)/shard_map/while/body/eval_jaxpr/grk,gkq->grq/dot_general | solution.py:68
  226.9 17.6 %copy.25 = f32[128,256,128]{0,2,1:T(8,128)} copy(f32[128,256,128]{2,1,0:T(8,128)} %fusion.105) | data formatting | bytes 33554432 | tf_op jit(solution)/shard_map/while/body/eval_jaxpr/grk,gkq->grq/dot_general | solution.py:68
  244.5 12.6 %fusion.106 = (f32[128,1,64,2,1,64]{0,5,4,3,2,1:T(8,128)}, f32[128,1,64,2,1,64]{0,5,4,3,2,1:T(8,128)}, f32[128,1,64,2,1,64]{0,5,4,3,2,1:T(8,128)}, f32[128,1,64,2,1,64]{0,5,4,3,2,1:T(8,128)}) fusion(f32[128,2,64,2,2,64]{0,5,4,3,2,1:T(8,128)} %bitcast.96), kind=kLoop, calls=%fused_computation.110.clone.1 | loop fusion | bytes 33554432 | tf_op jit(solution)/shard_map/while/body/eval_jaxpr/slice | solution.py:119
  257.0 0.7 add_bitcast_fusion.3
  258.4 4.9 %convolution_add_fusion.8 = f32[45,8192]{1,0:T(8,128)S(1)} fusion(f32[128,8192]{0,1:T(8,128)} %bitcast.101, f32[45,8192]{1,0:T(8,128)S(1)} %copy-done.3, pred[]{:T(512)S(6)} %compare.37, s32[128]{0:T(128)S(1)} %get-tuple-element.335, pred[128]{0:T(512)(128)(4,1)S(1)} %compare_bitcast_fusion.2), kind=kOutput, calls=%fused_computation.6.clone.1 | convolution fusion | flops 566979840 | bytes 7144065 | tf_op jit(solution)/shard_map/while/body/eval_jaxpr/dot_general | solution.py:120
  263.3 2.6 convolution_add_fusion.9
  265.9 2.6 convolution_add_fusion.10
  268.5 3.7 convolution_add_fusion.11
  272.2 0.7 fusion.103
  272.9 0.9 gather_fusion
  273.9 0.9 slice_negate_fusion.2
  274.8 5.7 %fusion.104 = bf16[128,128,128]{2,1,0:T(8,128)(2,1)} fusion(bf16[128,64,64]{2,1,0:T(8,128)(2,1)S(1)} %get-tuple-element.330, bf16[128,64,64]{2,1,0:T(8,128)(2,1)S(1)} %get-tuple-element.331, bf16[128,64,128]{2,1,0:T(8,128)(2,1)S(1)} %gather_fusion, bf16[3,128,128,128]{3,2,1,0:T(8,128)(2,1)} %get-tuple-element.369, s32[]{:T(128)} %get-tuple-element.353), kind=kOutput, calls=%fused_computation.15.clone.1 | convolution fusion | flops 551550976 | bytes 12583424 | tf_op jit(solution)/shard_map/while/body/eval_jaxpr/gpc,gcd->gpd/dot_general | solution.py:64
  280.5 6.9 %copy.23 = bf16[128,128,128]{0,2,1:T(8,128)(2,1)} copy(bf16[128,128,128]{2,1,0:T(8,128)(2,1)} %fusion.104) | data formatting | bytes 8388608 | tf_op jit(solution)/shard_map/while/body/eval_jaxpr/convert_element_type | solution.py:66
  287.3 7.4 %copy.24 = bf16[128,256,64]{1,2,0:T(8,128)(2,1)} copy(bf16[128,256,64]{0,2,1:T(8,128)(2,1)} %bitcast.97) | data formatting | bytes 8388608 | tf_op jit(solution)/shard_map/while/body/eval_jaxpr/reshape | solution.py:67
  294.8 11.0 %fusion.105 = f32[128,256,128]{2,1,0:T(8,128)} fusion(bf16[128,256,64]{1,2,0:T(8,128)(2,1)} %copy.24, bf16[3,128,64,128]{3,2,1,0:T(8,128)(2,1)} %get-tuple-element.372, s32[]{:T(128)} %get-tuple-element.353), kind=kOutput, calls=%fused_computation.17.clone.1 | convolution fusion | flops 536870912 | bytes 23069184 | tf_op jit(solution)/shard_map/while/body/eval_jaxpr/grk,gkq->grq/dot_general | solution.py:68
  305.7 17.6 %copy.25 = f32[128,256,128]{0,2,1:T(8,128)} copy(f32[128,256,128]{2,1,0:T(8,128)} %fusion.105) | data formatting | bytes 33554432 | tf_op jit(solution)/shard_map/while/body/eval_jaxpr/grk,gkq->grq/dot_general | solution.py:68
  323.3 12.6 %fusion.106 = (f32[128,1,64,2,1,64]{0,5,4,3,2,1:T(8,128)}, f32[128,1,64,2,1,64]{0,5,4,3,2,1:T(8,128)}, f32[128,1,64,2,1,64]{0,5,4,3,2,1:T(8,128)}, f32[128,1,64,2,1,64]{0,5,4,3,2,1:T(8,128)}) fusion(f32[128,2,64,2,2,64]{0,5,4,3,2,1:T(8,128)} %bitcast.96), kind=kLoop, calls=%fused_computation.110.clone.1 | loop fusion | bytes 33554432 | tf_op jit(solution)/shard_map/while/body/eval_jaxpr/slice | solution.py:119
  335.9 0.7 add_bitcast_fusion.3
  337.3 4.9 %convolution_add_fusion.8 = f32[45,8192]{1,0:T(8,128)S(1)} fusion(f32[128,8192]{0,1:T(8,128)} %bitcast.101, f32[45,8192]{1,0:T(8,128)S(1)} %copy-done.3, pred[]{:T(512)S(6)} %compare.37, s32[128]{0:T(128)S(1)} %get-tuple-element.335, pred[128]{0:T(512)(128)(4,1)S(1)} %compare_bitcast_fusion.2), kind=kOutput, calls=%fused_computation.6.clone.1 | convolution fusion | flops 566979840 | bytes 7144065 | tf_op jit(solution)/shard_map/while/body/eval_jaxpr/dot_general | solution.py:120
  342.2 2.6 convolution_add_fusion.9
  344.8 2.6 convolution_add_fusion.10
  347.4 3.7 convolution_add_fusion.11
  351.1 3.4 reshape.270
  354.6 5.1 %copy.18 = f32[5,9,64,2,64]{2,0,4,1,3:T(8,128)} copy(f32[5,9,64,2,64]{4,3,2,1,0:T(2,128)S(1)} %reshape.270) | data formatting | bytes 2949120 | tf_op jit(solution)/shard_map/reshape | solution.py:132
  359.7 3.5 reshape.271
  363.2 3.4 collective-permute-start
  366.6 5.9 %collective-permute-done = bf16[2,64,576]{1,2,0:T(8,128)(2,1)S(1)} collective-permute-done((bf16[2,64,576]{1,2,0:T(8,128)(2,1)S(1)}, bf16[2,64,576]{1,2,0:T(8,128)(2,1)S(1)}, u32[]{:S(2)}, u32[]{:S(2)}) %collective-permute-start) | collective-permute-done | bytes 147488 | tf_op jit(solution)/shard_map/ppermute | solution.py:16
  372.5 7.2 %scatter-add.6 = f32[2,320,576]{1,2,0:T(8,128)S(1)} dynamic-update-slice(f32[2,320,576]{1,2,0:T(8,128)S(1)} %reshape.271, f32[2,64,576]{1,2,0:T(8,128)S(1)} %slice_add_fusion.1, s32[]{:T(128)} %constant.151.clone.1, s32[]{:T(128)} %constant.151.clone.1, s32[]{:T(128)} %constant.151.clone.1) | dynamic-update-slice | bytes 589828 | tf_op jit(solution)/shard_map/scatter-add | solution.py:136
  379.8 1.3 collective-permute-start.1
  381.2 0.8 collective-permute-done.1
  382.0 1.3 copy.19
  (57 shorter events, 3.8 us)
Async XLA Ops:
  0.0 3.6 copy-start.4
  77.5 1.1 copy-start.5
  77.5 1.3 copy-start.6
  80.9 33.5 %all-to-all-start = ((bf16[32,2,64,128]{3,2,1,0:T(8,128)(2,1)}), bf16[32,2,64,128]{3,2,1,0:T(8,128)(2,1)S(1)}, u32[]{:S(2)}, u32[]{:S(2)}) async-start(bf16[32,2,64,128]{3,2,1,0:T(8,128)(2,1)} %broadcast_select_fusion), calls=%async_computation | async-start | bytes 2097152 | tf_op jit(solution)/shard_map/all_to_all | solution.py:93
  165.6 14.0 %copy-start.3 = (f32[45,8192]{1,0:T(8,128)S(1)}, f32[45,8192]{1,0:T(8,128)}, u32[]{:S(2)}) copy-start(f32[45,8192]{1,0:T(8,128)} %get-tuple-element.354) | copy-start | bytes 4423684 | tf_op jit(solution)/shard_map/while
  179.5 4.9 %copy-start.2 = (f32[128,1,64,2,1,64]{0,5,4,3,2,1:T(8,128)S(1)}, f32[128,1,64,2,1,64]{0,5,4,3,2,1:T(8,128)}, u32[]{:S(2)}) copy-start(f32[128,1,64,2,1,64]{0,5,4,3,2,1:T(8,128)} %get-tuple-element.336) | copy-start | bytes 12582916 | tf_op jit(solution)/shard_map/while
  184.4 2.6 copy-start.1
  187.0 2.6 copy-start
  244.5 14.0 %copy-start.3 = (f32[45,8192]{1,0:T(8,128)S(1)}, f32[45,8192]{1,0:T(8,128)}, u32[]{:S(2)}) copy-start(f32[45,8192]{1,0:T(8,128)} %get-tuple-element.354) | copy-start | bytes 4423684 | tf_op jit(solution)/shard_map/while
  258.4 4.9 %copy-start.2 = (f32[128,1,64,2,1,64]{0,5,4,3,2,1:T(8,128)S(1)}, f32[128,1,64,2,1,64]{0,5,4,3,2,1:T(8,128)}, u32[]{:S(2)}) copy-start(f32[128,1,64,2,1,64]{0,5,4,3,2,1:T(8,128)} %get-tuple-element.336) | copy-start | bytes 12582916 | tf_op jit(solution)/shard_map/while
  263.3 2.6 copy-start.1
  265.9 2.6 copy-start
  323.3 14.0 %copy-start.3 = (f32[45,8192]{1,0:T(8,128)S(1)}, f32[45,8192]{1,0:T(8,128)}, u32[]{:S(2)}) copy-start(f32[45,8192]{1,0:T(8,128)} %get-tuple-element.354) | copy-start | bytes 4423684 | tf_op jit(solution)/shard_map/while
  337.3 4.9 %copy-start.2 = (f32[128,1,64,2,1,64]{0,5,4,3,2,1:T(8,128)S(1)}, f32[128,1,64,2,1,64]{0,5,4,3,2,1:T(8,128)}, u32[]{:S(2)}) copy-start(f32[128,1,64,2,1,64]{0,5,4,3,2,1:T(8,128)} %get-tuple-element.336) | copy-start | bytes 12582916 | tf_op jit(solution)/shard_map/while
  342.2 2.6 copy-start.1
  344.8 2.6 copy-start
  363.2 9.3 %collective-permute-start = (bf16[2,64,576]{1,2,0:T(8,128)(2,1)S(1)}, bf16[2,64,576]{1,2,0:T(8,128)(2,1)S(1)}, u32[]{:S(2)}, u32[]{:S(2)}) collective-permute-start(bf16[2,64,576]{1,2,0:T(8,128)(2,1)S(1)} %slice.187), channel_id=1, source_target_pairs={{0,4},{4,8},{8,12},{12,16},{16,20},{20,24},{24,28},{1,5},{5,9},{9,... | collective-permute-start | bytes 442376 | tf_op jit(solution)/shard_map/ppermute | solution.py:16
  379.8 2.2 collective-permute-start.1
where the time goes:
time: 389 us; the launch traced here: 383 us
  local copies, waits for them, and re-layouts  158 us (41%)
  matrix products  98.7 us (25%)
  other arithmetic  81.3 us (21%)
  waiting for transfers between devices  32.9 us (8%)
  starting transfers between devices  12 us (3%)
    convert_element_type x1, other arithmetic, aperture_screens(): real_part = (magnitude * jnp.cos(angles)).astype(jnp.bfloat16)  61.6 us
    dot_general x3, local copies, waits for them, and re-layouts, grid_patches(): jnp.einsum('grk,gkq->grq', stacked_rows, right_rows, preferred_element_ty...  52.8 us
    dot_general x12, matrix products, grid_group(): placed = placed + jnp.dot(onehot, piece, precision=lax.Precision.HIGHEST)  41.2 us
    slice x3, local copies, waits for them, and re-layouts, grid_group(): piece = quarters[:, row_half, :, :, col_half, :].reshape(group_size, -1)  37.7 us
    dot_general x3, matrix products, grid_patches(): jnp.einsum('grk,gkq->grq', stacked_rows, right_rows, preferred_element_ty...  33 us
    all_to_all x1, waiting for transfers between devices, shards(): lax.all_to_all(outgoing, ('tu', 'tv'), split_axis=0, concat_axis=0, tiled...  26.2 us
    reshape x3, local copies, waits for them, and re-layouts, grid_patches(): mixed.reshape(mixed.shape[0], 2 * mixed.shape[1], kernel_size)  22.2 us
    convert_element_type x3, local copies, waits for them, and re-layouts, grid_patches(): mixed = jnp.einsum('gpc,gcd->gpd', left_rows, operator_rows, preferred_el...  20.6 us
  transfers between devices with their start and end apart: 3, of which 3 were waited for; matrix products, arithmetic and copies ran while one was open for 0% of the time, Pallas kernels for 0%

commit v1 on v0

v1 whole, which is shorter than its diff:
```python
import functools
import math

import jax
import jax.numpy as jnp
import numpy as np
from jax import lax
from jax.experimental import pallas as pl
from jax.experimental.pallas import tpu as pltpu
from jax.sharding import PartitionSpec as P

TILE_U = 256
TILE_V = 512
QUAD = 4
UNROLL = 4
SPLIT = 1

def _fit(fn, degree):
    span = math.pi ** 2
    nodes = 0.5 * span * (1.0 - np.cos(np.pi * (np.arange(400) + 0.5) / 400))
    cheb = np.polynomial.chebyshev.Chebyshev.fit(nodes, fn(np.sqrt(nodes)), degree, domain=[0, span])
    return [float(c) for c in cheb.convert(kind=np.polynomial.Polynomial).coef]


COS_POLY = _fit(np.cos, 6)
SIN_POLY = _fit(lambda x: np.sin(x) / x, 5)


def horner(coefs, u):
    total = jnp.full_like(u, coefs[-1])
    for coef in coefs[-2::-1]:
        total = total * u + coef
    return total


def cos_sin(x):
    u = x * x
    return horner(COS_POLY, u), x * horner(SIN_POLY, u)


def from_behind(block, axis, distance):
    devices = range(lax.axis_size(axis))
    route = [(i - distance, i) for i in devices if i - distance in devices]
    return lax.ppermute(block, axis, route)


def in_hbm(array):
    return pltpu.with_memory_space_constraint(array, pltpu.HBM)


def in_vmem(array):
    return pltpu.with_memory_space_constraint(array, pltpu.VMEM)


def kernels_body(
    list_hbm, depth_hbm, amp_hbm, phase_hbm, out_ref,
    chosen_list, depth, amp, phase, table, screen, halves, made, small_sems, bulk_sems,
):
    screens, size, _ = amp.shape
    planes = depth.shape[0]
    kernel_size = out_ref.shape[1]
    small = [
        pltpu.make_async_copy(depth_hbm, depth, small_sems.at[0]),
        pltpu.make_async_copy(list_hbm, chosen_list, small_sems.at[1]),
    ]
    for copy in small:
        copy.start()

    def bulk(s):
        return [
            pltpu.make_async_copy(amp_hbm.at[s], amp.at[s], bulk_sems.at[0, s]),
            pltpu.make_async_copy(phase_hbm.at[s], phase.at[s], bulk_sems.at[1, s]),
        ]

    for s in range(screens):
        for copy in bulk(s):
            copy.start()

    frequency = lax.broadcasted_iota(jnp.int32, (kernel_size, size), 0) - kernel_size // 2
    cells = lax.broadcasted_iota(jnp.int32, (kernel_size, size), 1)
    turns = frequency.astype(jnp.float32) * cells.astype(jnp.float32) / size
    real_f, imag_f = cos_sin((2.0 * math.pi) * (turns - jnp.round(turns)))
    real_f = real_f.astype(jnp.bfloat16).astype(jnp.float32)
    imag_f = (-imag_f).astype(jnp.bfloat16).astype(jnp.float32)
    place = (lax.broadcasted_iota(jnp.int32, (1, size), 1).astype(jnp.float32) - size // 2) / size
    square = place * place
    for copy in small:
        copy.wait()
    for p in range(planes):
        turns = depth[p] * square
        real_e, imag_e = cos_sin((2.0 * math.pi) * (turns - jnp.round(turns)))
        real_g = (real_f * real_e - imag_f * imag_e).astype(jnp.bfloat16)
        imag_g = (real_f * imag_e + imag_f * real_e).astype(jnp.bfloat16)
        top = slice(p * 2 * kernel_size, (p * 2 + 1) * kernel_size)
        low = slice((p * 2 + 1) * kernel_size, (p * 2 + 2) * kernel_size)
        table[top, :size] = real_g
        table[top, size:] = -imag_g
        table[low, :size] = imag_g
        table[low, size:] = real_g

    width = 256

    @pl.loop(0, screens)
    def _(s):
        for copy in bulk(s):
            copy.wait()
        for start in range(0, size, width):
            cols = slice(start, start + width)
            magnitude = amp[s, :, cols].astype(jnp.float32)
            real_e, imag_e = cos_sin(phase[s, :, cols].astype(jnp.float32))
            screen[:size, cols] = (magnitude * real_e).astype(jnp.bfloat16)
            screen[size:, cols] = (magnitude * imag_e).astype(jnp.bfloat16)
            product = jnp.dot(table[...], screen[:, cols], preferred_element_type=jnp.float32)
            for p in range(planes):
                base = p * 2 * kernel_size
                halves[p, :, start : start + width] = product[base : base + kernel_size].astype(jnp.bfloat16)
                halves[p, :, size + start : size + start + width] = product[
                    base + kernel_size : base + 2 * kernel_size
                ].astype(jnp.bfloat16)
        for p in range(planes):
            second = lax.dot_general(
                halves[p],
                table[p * 2 * kernel_size : (p + 1) * 2 * kernel_size, :],
                (((1,), (1,)), ((), ())),
                preferred_element_type=jnp.float32,
            )
            made[s * planes + p] = (second * (1.0 / size)).astype(jnp.bfloat16)

    capacity, tiles = chosen_list.shape

    @pl.loop(0, tiles)
    def _(t):
        for c in range(capacity):
            which = chosen_list[c, t]
            chosen = made[jnp.maximum(which, 0)]
            out_ref[t * capacity + c] = jnp.where(which >= 0, chosen, jnp.zeros_like(chosen))


def make_kernels(aperture_amp, aperture_phase, plane_depths, chosen_list, kernel_size):
    screens, size, _ = aperture_amp.shape
    planes = plane_depths.shape[0]
    capacity, tiles = chosen_list.shape
    hbm = pl.BlockSpec(memory_space=pl.ANY)
    return pl.pallas_call(
        kernels_body,
        in_specs=[hbm] * 4,
        out_specs=pl.BlockSpec(memory_space=pltpu.VMEM),
        out_shape=jax.ShapeDtypeStruct((tiles * capacity, kernel_size, 2 * kernel_size), jnp.bfloat16),
        scratch_shapes=[
            pltpu.SMEM((capacity, tiles), jnp.int32),
            pltpu.SMEM((planes,), jnp.float32),
            pltpu.VMEM((screens, size, size), jnp.bfloat16),
            pltpu.VMEM((screens, size, size), jnp.bfloat16),
            pltpu.VMEM((planes * 2 * kernel_size, 2 * size), jnp.bfloat16),
            pltpu.VMEM((2 * size, size), jnp.bfloat16),
            pltpu.VMEM((planes, kernel_size, 2 * size), jnp.bfloat16),
            pltpu.VMEM((screens * planes, kernel_size, 2 * kernel_size), jnp.bfloat16),
            pltpu.SemaphoreType.DMA((2,)),
            pltpu.SemaphoreType.DMA((2, screens)),
        ],
        compiler_params=pltpu.CompilerParams(vmem_limit_bytes=32 * 2**20),
        name="make_kernels",
    )(in_hbm(chosen_list), in_hbm(plane_depths), in_hbm(aperture_amp), in_hbm(aperture_phase))


class Layout:
    def __init__(self, blocks, anchors):
        step = 2 * UNROLL
        self.parts = SPLIT + 1
        buckets = SPLIT * anchors
        self.quads = (blocks + (QUAD - 1) * buckets) // QUAD + 1 + self.parts * (step - 1) + UNROLL
        self.anchor = self.parts + 1
        self.block = self.anchor + self.quads
        self.slot = self.block + self.quads * QUAD
        self.total = self.slot + self.quads * QUAD


def plan_body(
    pos_ref, slot_ref, count_ref, half_ref, left_hbm, right_hbm, plan_ref, left_ref, right_ref,
    tally, cursor, sems, *, row_slots, col_slots, half_slots,
):
    copies = [
        pltpu.make_async_copy(left_hbm, left_ref, sems.at[0]),
        pltpu.make_async_copy(right_hbm, right_ref, sems.at[1]),
    ]
    for copy in copies:
        copy.start()
    anchors = row_slots * col_slots
    border = row_slots + col_slots - 1
    layout = Layout(pos_ref.shape[0], anchors)
    step = 2 * UNROLL

    @pl.loop(0, SPLIT * anchors)
    def _(b):
        tally[b] = 0

    live = count_ref[0]

    def bucket_of(j):
        q = pos_ref[j]
        row = q // col_slots
        col = q % col_slots
        rank = jnp.where(
            row == row_slots - 1,
            col,
            jnp.where(
                col == col_slots - 1, col_slots + row, border + row * (col_slots - 1) + col
            ),
        )
        if SPLIT == 1:
            return rank
        other = (slot_ref[j] // half_slots) != half_ref[0]
        return rank + jnp.where(other, anchors, 0)

    @pl.loop(0, live)
    def _(j):
        b = bucket_of(j)
        tally[b] = tally[b] + 1

    def dead(quad):
        plan_ref[layout.anchor + quad] = 0
        for e in range(QUAD):
            plan_ref[layout.block + quad * QUAD + e] = 0
            plan_ref[layout.slot + quad * QUAD + e] = -1

    def lay(b, quad):
        rank = lax.rem(b, anchors)
        inner = rank - border
        q = jnp.where(
            rank < col_slots,
            (row_slots - 1) * col_slots + rank,
            jnp.where(
                rank < border,
                (rank - col_slots) * col_slots + col_slots - 1,
                (inner // (col_slots - 1)) * col_slots + lax.rem(inner, col_slots - 1),
            ),
        )
        number = tally[b]
        quads = (number + QUAD - 1) // QUAD
        cursor[b] = quad * QUAD

        @pl.loop(0, quads)
        def _(i):
            plan_ref[layout.anchor + quad + i] = q

        @pl.loop(quad * QUAD + number, (quad + quads) * QUAD)
        def _(i):
            plan_ref[layout.block + i] = 0
            plan_ref[layout.slot + i] = -1

        return quad + quads

    ends = [border, anchors] if SPLIT == 1 else [anchors, anchors + border, 2 * anchors]
    quad = 0
    begin = 0
    plan_ref[0] = 0
    for part, end in enumerate(ends):
        quad = lax.fori_loop(begin, end, lay, quad)
        begin = end
        full = ((quad + step - 1) // step) * step
        pl.loop(quad, full)(dead)
        quad = full
        plan_ref[part + 1] = quad
    pl.loop(quad, quad + UNROLL)(dead)

    @pl.loop(0, live)
    def _(j):
        b = bucket_of(j)
        at = cursor[b]
        cursor[b] = at + 1
        plan_ref[layout.block + at] = j
        slot = slot_ref[j]
        plan_ref[layout.slot + at] = slot if SPLIT == 1 else lax.rem(slot, half_slots)

    for copy in copies:
        copy.wait()


def plan_blocks(block_pos, block_slot, block_count, half, vis_left, vis_right, half_slots):
    kernel_size = vis_right.shape[1]
    row_slots, col_slots = TILE_U // kernel_size, TILE_V // kernel_size
    layout = Layout(block_pos.shape[0], row_slots * col_slots)
    smem = pl.BlockSpec(memory_space=pltpu.SMEM)
    hbm = pl.BlockSpec(memory_space=pl.ANY)
    vmem = pl.BlockSpec(memory_space=pltpu.VMEM)
    return pl.pallas_call(
        functools.partial(
            plan_body, row_slots=row_slots, col_slots=col_slots, half_slots=half_slots
        ),
        in_specs=[smem] * 4 + [hbm] * 2,
        out_specs=[smem, vmem, vmem],
        out_shape=[
            jax.ShapeDtypeStruct((layout.total,), jnp.int32),
            pltpu.VMEM(vis_left.shape, vis_left.dtype),
            pltpu.VMEM(vis_right.shape, vis_right.dtype),
        ],
        scratch_shapes=[
            pltpu.SMEM((SPLIT * row_slots * col_slots,), jnp.int32),
            pltpu.SMEM((SPLIT * row_slots * col_slots,), jnp.int32),
            pltpu.SemaphoreType.DMA((2,)),
        ],
        compiler_params=pltpu.CompilerParams(vmem_limit_bytes=2**20),
        name="plan_blocks",
    )(block_pos, block_slot, block_count, half, in_hbm(vis_left), in_hbm(vis_right))


def strip(sums, row_slots, col_slots, kernel_size, plane, a, col):
    patch = sums.shape[1]
    lanes = slice(plane * patch, (plane + 1) * patch)
    total = None
    if a < row_slots:
        total = sums[a * col_slots + col, :kernel_size, lanes]
    if a > 0:
        above = sums[(a - 1) * col_slots + col, kernel_size:, lanes]
        total = above if total is None else total + above
    return total


def grid_body(
    plan_ref, kern_ref, left_ref, right_ref, *rest, part, first_part, halo, row_slots, col_slots
):
    if first_part:
        sums, *rest = rest
    else:
        before, sums, *rest = rest
    if halo:
        row_ref, col_ref, corner_ref, *rest = rest
    mixed = rest
    slots, kernel_size, _ = kern_ref.shape
    blocks, patch, _ = left_ref.shape
    anchors = sums.shape[0]
    layout = Layout(blocks, anchors)
    if first_part:

        @pl.loop(0, anchors)
        def _(q):
            sums[q] = jnp.zeros(sums.shape[1:], sums.dtype)

    zero = jnp.zeros((kernel_size, patch), jnp.bfloat16)

    def first(quad, ref, u):
        for e in range(QUAD):
            at = quad * QUAD + e
            slot = plan_ref[layout.slot + at]
            right = right_ref[plan_ref[layout.block + at]]
            kern = kern_ref[jnp.maximum(slot, 0)]
            kern = jnp.where(slot >= 0, kern, jnp.zeros_like(kern))
            spread = jnp.concatenate(
                [jnp.concatenate([right, zero], axis=1), jnp.concatenate([zero, right], axis=1)], axis=0
            )
            out = jnp.dot(kern, spread, preferred_element_type=jnp.float32).astype(jnp.bfloat16)
            top = slice(e * 2 * kernel_size, (e * 2 + 1) * kernel_size)
            low = slice((e * 2 + 1) * kernel_size, (e * 2 + 2) * kernel_size)
            ref[u, top, :] = out
            ref[u, low, :patch] = -out[:, patch:]
            ref[u, low, patch:] = out[:, :patch]

    def second(quad, ref, u):
        left = jnp.concatenate(
            [left_ref[plan_ref[layout.block + quad * QUAD + e]] for e in range(QUAD)], axis=1
        )
        sums[plan_ref[layout.anchor + quad]] += jnp.dot(left, ref[u], preferred_element_type=jnp.float32)

    begin = plan_ref[part]
    end = plan_ref[part + 1]
    for u in range(UNROLL):
        first(begin + u, mixed[0], u)

    @pl.loop(0, (end - begin) // (2 * UNROLL))
    def _(i):
        for h in range(2):
            quad = begin + (2 * i + h) * UNROLL
            for u in range(UNROLL):
                first(quad + UNROLL + u, mixed[1 - h], u)
                second(quad + u, mixed[h], u)

    if not halo:
        return
    low = lax.broadcasted_iota(jnp.int32, (kernel_size, patch), 1) < kernel_size
    take = functools.partial(strip, sums, row_slots, col_slots, kernel_size)
    for plane in range(2):
        behind = 0.0
        for tile in range(col_slots // 2):
            even = take(plane, row_slots, 2 * tile)
            odd = pltpu.roll(take(plane, row_slots, 2 * tile + 1), kernel_size, 1)
            row_ref[plane, :, tile * patch : (tile + 1) * patch] = (
                even + jnp.where(low, behind, odd)
            ).astype(row_ref.dtype)
            behind = odd
    for a in range(row_slots + 1):
        real = pltpu.roll(take(0, a, col_slots - 1), kernel_size, 1)
        imag = take(1, a, col_slots - 1)
        edge = jnp.where(low, real, imag)
        if a < row_slots:
            col_ref[a * kernel_size : (a + 1) * kernel_size, :] = edge.astype(col_ref.dtype)
        else:
            corner_ref[...] = edge.astype(corner_ref.dtype)


def grid_part(plan, part, kernels, left, right, sums, halo):
    kernel_size = kernels.shape[1]
    patch = left.shape[1]
    row_slots, col_slots = TILE_U // kernel_size, TILE_V // kernel_size
    smem = pl.BlockSpec(memory_space=pltpu.SMEM)
    vmem = pl.BlockSpec(memory_space=pltpu.VMEM)
    first_part = sums is None
    operands = [plan, in_vmem(kernels), in_vmem(left), in_vmem(right)]
    if not first_part:
        operands.append(in_vmem(sums))
    out_shape = [pltpu.VMEM((row_slots * col_slots, patch, 2 * patch), jnp.float32)]
    if halo:
        out_shape += [
            jax.ShapeDtypeStruct((2, kernel_size, TILE_V), jnp.bfloat16),
            jax.ShapeDtypeStruct((TILE_U, 2 * kernel_size), jnp.bfloat16),
            jax.ShapeDtypeStruct((kernel_size, 2 * kernel_size), jnp.bfloat16),
        ]
    return pl.pallas_call(
        functools.partial(
            grid_body, part=part, first_part=first_part, halo=halo, row_slots=row_slots, col_slots=col_slots
        ),
        in_specs=[smem] + [vmem] * (len(operands) - 1),
        out_specs=[vmem] * len(out_shape),
        out_shape=out_shape,
        input_output_aliases={} if first_part else {4: 0},
        scratch_shapes=[pltpu.VMEM((UNROLL, QUAD * 2 * kernel_size, 2 * patch), jnp.bfloat16)] * 2,
        compiler_params=pltpu.CompilerParams(vmem_limit_bytes=12 * 2**20),
        name="grid_part",
    )(*operands)


def merge_body(sums, row_ref, col_ref, corner_ref, out_ref):
    kernel_size = row_ref.shape[1]
    patch = sums.shape[1]
    row_slots = out_ref.shape[1] // kernel_size
    col_slots = out_ref.shape[2] // kernel_size
    low = lax.broadcasted_iota(jnp.int32, (kernel_size, patch), 1) < kernel_size
    take = functools.partial(strip, sums, row_slots, col_slots, kernel_size)
    for a in range(row_slots):
        rows = slice(a * kernel_size, (a + 1) * kernel_size)
        edge = col_ref[rows, :].astype(jnp.float32)
        if a == 0:
            edge = edge + corner_ref[...].astype(jnp.float32)
        for plane in range(2):
            behind = edge if plane == 0 else pltpu.roll(edge, kernel_size, 1)
            for tile in range(col_slots // 2):
                lanes = slice(tile * patch, (tile + 1) * patch)
                odd = pltpu.roll(take(plane, a, 2 * tile + 1), kernel_size, 1)
                value = take(plane, a, 2 * tile) + jnp.where(low, behind, odd)
                if a == 0:
                    value = value + row_ref[plane, :, lanes].astype(jnp.float32)
                out_ref[plane, rows, lanes] = value
                behind = odd


def merge_tile(sums, row, col, corner):
    vmem = pl.BlockSpec(memory_space=pltpu.VMEM)
    return pl.pallas_call(
        merge_body,
        in_specs=[vmem] * 4,
        out_specs=vmem,
        out_shape=jax.ShapeDtypeStruct((2, TILE_U, TILE_V), jnp.float32),
        compiler_params=pltpu.CompilerParams(vmem_limit_bytes=8 * 2**20),
        name="merge_tile",
    )(in_vmem(sums), row, col, corner)


def shards(
    aperture_amp,
    aperture_phase,
    plane_depths,
    send_list,
    send_count,
    vis_left,
    vis_right,
    block_slot,
    block_pos,
    block_count,
):
    kernel_size = vis_right.shape[1]
    tiles, capacity = send_list.shape[1:]
    both = ("tu", "tv")
    used = jnp.arange(capacity, dtype=jnp.int32)[:, None] < send_count
    chosen_list = jnp.where(used, send_list[0].T, -1)
    outgoing = make_kernels(aperture_amp, aperture_phase, plane_depths, chosen_list, kernel_size)
    outgoing = outgoing.reshape((tiles, capacity) + outgoing.shape[1:])
    arrived = lax.all_to_all(outgoing, both, split_axis=0, concat_axis=0, tiled=True)
    received = arrived.reshape((-1,) + arrived.shape[2:])
    half = jnp.zeros((1,), jnp.int32)
    plan, left, right = plan_blocks(
        block_pos, block_slot, block_count, half, vis_left, vis_right, tiles * capacity
    )
    sums, row, col, corner = grid_part(plan, 0, received, left, right, None, True)
    row = from_behind(row, "tu", 1)
    col = from_behind(col, "tv", 1)
    rows, cols = lax.axis_size("tu"), lax.axis_size("tv")
    diagonal = [
        (i * cols + j, (i + 1) * cols + j + 1) for i in range(rows - 1) for j in range(cols - 1)
    ]
    corner = lax.ppermute(corner, both, diagonal)
    (sums,) = grid_part(plan, 1, received, left, right, sums, False)
    return merge_tile(sums, row, col, corner)


def solution(mesh):
    placed = (
        P(("tu", "tv"), None, None),
        P(("tu", "tv"), None, None),
        P(),
        P(("tu", "tv"), None, None),
        P(("tu", "tv"), None),
        P(("tu", "tv"), None, None),
        P(("tu", "tv"), None, None),
        P(("tu", "tv")),
        P(("tu", "tv")),
        P(("tu", "tv")),
    )
    return jax.shard_map(
        shards, mesh=mesh, in_specs=placed, out_specs=P(None, "tu", "tv"), check_vma=False
    )
```

time: 389 us -> 73.6 us (0.19)
  the two profiles are of different devices: /device:TPU:0 before, /device:TPU:19 now
where the time goes in v1:
time: 73.6 us; the launch traced here: 73.5 us
  Pallas kernels  39.7 us (54%)
  starting transfers between devices  17.4 us (24%)
  local copies, waits for them, and re-layouts  14.5 us (20%)
  other arithmetic  1.24 us (2%)
  between operations  0.76 us (1%)
    pallas_call x1, Pallas kernels, plan_blocks(): pl.pallas_call(functools.partial(plan_body, row_slots=row_slots, col_slot...  16.5 us
    unnamed x12, local copies, waits for them, and re-layouts  14.5 us
    pallas_call x2, Pallas kernels, grid_part(): pl.pallas_call(functools.partial(grid_body, part=part, first_part=first_p...  12.6 us
    pallas_call x1, Pallas kernels, make_kernels(): pl.pallas_call(kernels_body, in_specs=[hbm] * 4, out_specs=pl.BlockSpec(m...  9.19 us
    ppermute x2, starting transfers between devices, from_behind(): return lax.ppermute(block, axis, route)  7.45 us
    all_to_all x1, starting transfers between devices, shards(): lax.all_to_all(outgoing, both, split_axis=0, concat_axis=0, tiled=True)  6.24 us
    ppermute x1, starting transfers between devices, shards(): corner = lax.ppermute(corner, both, diagonal)  3.68 us
  transfers between devices with their start and end apart: 4, of which 0 were waited for; matrix products, arithmetic and copies ran while one was open for 0% of the time, Pallas kernels for 32%

profile of v1, /device:TPU:19, one launch (start us, length us, event | category | flops | bytes accessed | tf_op | source)
XLA Modules:
  0.0 73.5 jit_solution(13394860809214404959)
XLA Ops:
  0.0 0.0 copy-start.4
  0.0 0.0 copy-start.5
  0.0 1.2 %compare_select_fusion.list_hbm = s32[2,32]{1,0:T(2,128)} fusion(s32[1,32,2]{1,2,0:T(2,128)} %param.13, s32[32]{0:T(128)} %bitcast.9), kind=kLoop, calls=%fused_computation | loop fusion | flops 128 | bytes 640 | tf_op jit(solution)/shard_map/jit(_where)/select_n | solution.py:483
  1.2 9.2 %make_kernels.1 = bf16[64,64,128]{2,1,0:T(8,128)(2,1)} custom-call(s32[2,32]{1,0:T(2,128)} %compare_select_fusion.list_hbm, f32[4]{0:T(128)} %depth_hbm.1, bf16[4,512,512]{2,1,0:T(8,128)(2,1)} %amp_hbm.1, bf16[4,512,512]{2,1,0:T(8,128)(2,1)} %phase_hbm.1), custom_call_target="tpu_custom_call" | custom-call | tf_op jit(solution)/shard_map/make_kernels/pallas_call | solution.py:144
  10.4 6.2 %all-to-all-start = ((bf16[32,2,64,128]{3,2,1,0:T(8,128)(2,1)}), bf16[32,2,64,128]{3,2,1,0:T(8,128)(2,1)S(1)}, u32[]{:S(2)}, u32[]{:S(2)}) async-start(bf16[32,2,64,128]{3,2,1,0:T(8,128)(2,1)} %bitcast.3), calls=%async_computation | async-start | bytes 2097152 | tf_op jit(solution)/shard_map/all_to_all | solution.py:486
  17.3 0.0 copy-done.4
  17.3 0.0 copy-done.5
  17.4 16.5 %plan_blocks.1 = (s32[1254]{0:T(1024)S(1)}, bf16[384,128,128]{2,1,0:T(8,128)(2,1)S(1)}, bf16[384,64,128]{2,1,0:T(8,128)(2,1)S(1)}) custom-call(s32[384]{0:T(512)S(1)} %copy-done.4, s32[384]{0:T(512)S(1)} %copy-done.5, s32[1]{0:T(128)S(6)} %copy.13.count_ref, s32[1]{0:T(128)} %constant.0.clone.1.half_ref, bf16[384,128,128]{2,1,0:T(8,128)(2,1)} %left_hbm.1, ...), custom_call_target="tpu_custom_call" | custom-call | tf_op jit(solution)/shard_map/plan_blocks/pallas_call | solution.py:286
  33.9 0.0 copy-start
  33.9 4.5 %copy-done = bf16[384,128,128]{2,1,0:T(8,128)(2,1)} copy-done((bf16[384,128,128]{2,1,0:T(8,128)(2,1)}, bf16[384,128,128]{2,1,0:T(8,128)(2,1)S(1)}, u32[]{:S(2)}) %copy-start) | copy-done | bytes 12582936
  38.4 0.0 copy-start.2
  38.4 2.6 %copy-done.2 = bf16[384,64,128]{2,1,0:T(8,128)(2,1)} copy-done((bf16[384,64,128]{2,1,0:T(8,128)(2,1)}, bf16[384,64,128]{2,1,0:T(8,128)(2,1)S(1)}, u32[]{:S(2)}) %copy-start.2) | copy-done | bytes 6291480
  41.0 0.0 all-to-all-done
  41.0 0.0 copy-start.1
  41.0 4.6 %copy-done.1 = bf16[384,128,128]{2,1,0:T(8,128)(2,1)S(1)} copy-done((bf16[384,128,128]{2,1,0:T(8,128)(2,1)S(1)}, bf16[384,128,128]{2,1,0:T(8,128)(2,1)}, u32[]{:S(2)}) %copy-start.1) | copy-done | bytes 12582936
  45.6 0.0 copy-start.3
  45.6 2.8 %copy-done.3 = bf16[384,64,128]{2,1,0:T(8,128)(2,1)S(1)} copy-done((bf16[384,64,128]{2,1,0:T(8,128)(2,1)S(1)}, bf16[384,64,128]{2,1,0:T(8,128)(2,1)}, u32[]{:S(2)}) %copy-start.3) | copy-done | bytes 6291480
  48.4 5.4 %grid_part.2 = (f32[32,128,256]{2,1,0:T(8,128)S(1)}, bf16[2,64,512]{2,1,0:T(8,128)(2,1)S(1)}, bf16[256,128]{1,0:T(8,128)(2,1)S(1)}, bf16[64,128]{1,0:T(8,128)(2,1)S(1)}) custom-call(s32[1254]{0:T(1024)S(1)} %get-tuple-element.12.plan_ref, bf16[64,64,128]{2,1,0:T(8,128)(2,1)S(1)} %bitcast.7, bf16[384,128,128]{2,1,0:T(8,128)(2,1)S(1)} %copy-done.1, ...), custom_call_target="tpu_custom_call" | custom-call | tf_op jit(solution)/shard_map/grid_part/pallas_call | solution.py:417
  53.7 1.9 %collective-permute-start = (bf16[2,64,512]{2,1,0:T(8,128)(2,1)S(1)}, bf16[2,64,512]{2,1,0:T(8,128)(2,1)S(1)}, u32[]{:S(2)}, u32[]{:S(2)}) collective-permute-start(bf16[2,64,512]{2,1,0:T(8,128)(2,1)S(1)} %get-tuple-element.16), channel_id=1, source_target_pairs={{0,4},{4,8},{8,12},{12,16},{16,20},{20,24},{24,28},{1,5},{5,9},{9,... | collective-permute-start | bytes 393224 | tf_op jit(solution)/shard_map/ppermute | solution.py:44
  55.7 5.5 %collective-permute-start.1 = (bf16[256,128]{1,0:T(8,128)(2,1)S(1)}, bf16[256,128]{1,0:T(8,128)(2,1)S(1)}, u32[]{:S(2)}, u32[]{:S(2)}) collective-permute-start(bf16[256,128]{1,0:T(8,128)(2,1)S(1)} %get-tuple-element.17), channel_id=1, source_target_pairs={{0,1},{1,2},{2,3},{4,5},{5,6},{6,7},{8,9},{9,10},{10,11},{12,13},{... | collective-permute-start | bytes 196616 | tf_op jit(solution)/shard_map/ppermute | solution.py:44
  61.2 3.7 %collective-permute-start.2 = (bf16[64,128]{1,0:T(8,128)(2,1)S(1)}, bf16[64,128]{1,0:T(8,128)(2,1)S(1)}, u32[]{:S(2)}, u32[]{:S(2)}) collective-permute-start(bf16[64,128]{1,0:T(8,128)(2,1)S(1)} %get-tuple-element.18), channel_id=1, source_target_pairs={{0,5},{1,6},{2,7},{4,9},{5,10},{6,11},{8,13},{9,14},{10,15},{12,17... | collective-permute-start | bytes 49160 | tf_op jit(solution)/shard_map/ppermute | solution.py:499
  64.9 7.3 %grid_part.3.sums = f32[32,128,256]{2,1,0:T(8,128)S(1)} custom-call(s32[1254]{0:T(1024)S(1)} %get-tuple-element.12.plan_ref, bf16[64,64,128]{2,1,0:T(8,128)(2,1)S(1)} %bitcast.8, bf16[384,128,128]{2,1,0:T(8,128)(2,1)S(1)} %copy-done.1, bf16[384,64,128]{2,1,0:T(8,128)(2,1)S(1)} %copy-done.3, ...), custom_call_target="tpu_custom_call", output_to_operand_aliasing={{}: (4, {})} | custom-call | tf_op jit(solution)/shard_map/grid_part/pallas_call | solution.py:417
  72.2 0.0 collective-permute-done.2.corner_ref
  72.2 0.0 collective-permute-done.1.col_ref
  72.2 0.0 collective-permute-done.row_ref
  72.2 1.3 %merge_tile.1 = f32[2,256,512]{2,1,0:T(8,128)} custom-call(f32[32,128,256]{2,1,0:T(8,128)S(1)} %grid_part.3.sums, bf16[2,64,512]{2,1,0:T(8,128)(2,1)S(1)} %collective-permute-done.row_ref, bf16[256,128]{1,0:T(8,128)(2,1)S(1)} %collective-permute-done.1.col_ref, bf16[64,128]{1,0:T(8,128)(2,1)S(1)} %collective-permute-done.2.corner_ref), custom_call_target="tpu_custom_call" | custom-call | tf_op jit(solution)/shard_map/merge_tile/pallas_call | solution.py:457
Async XLA Ops:
  0.0 17.3 %copy-start.4 = (s32[384]{0:T(512)S(1)}, s32[384]{0:T(512)}, u32[]{:S(2)}) copy-start(s32[384]{0:T(512)} %pos_ref.1) | copy-start | bytes 4612
  0.0 17.3 %copy-start.5 = (s32[384]{0:T(512)S(1)}, s32[384]{0:T(512)}, u32[]{:S(2)}) copy-start(s32[384]{0:T(512)} %slot_ref.1) | copy-start | bytes 4612
  10.4 30.6 %all-to-all-start = ((bf16[32,2,64,128]{3,2,1,0:T(8,128)(2,1)}), bf16[32,2,64,128]{3,2,1,0:T(8,128)(2,1)S(1)}, u32[]{:S(2)}, u32[]{:S(2)}) async-start(bf16[32,2,64,128]{3,2,1,0:T(8,128)(2,1)} %bitcast.3), calls=%async_computation | async-start | bytes 2097152 | tf_op jit(solution)/shard_map/all_to_all | solution.py:486
  33.9 4.5 %copy-start = (bf16[384,128,128]{2,1,0:T(8,128)(2,1)}, bf16[384,128,128]{2,1,0:T(8,128)(2,1)S(1)}, u32[]{:S(2)}) copy-start(bf16[384,128,128]{2,1,0:T(8,128)(2,1)S(1)} %get-tuple-element.13.left_ref) | copy-start | bytes 37748740
  38.4 2.6 %copy-start.2 = (bf16[384,64,128]{2,1,0:T(8,128)(2,1)}, bf16[384,64,128]{2,1,0:T(8,128)(2,1)S(1)}, u32[]{:S(2)}) copy-start(bf16[384,64,128]{2,1,0:T(8,128)(2,1)S(1)} %get-tuple-element.14.right_ref) | copy-start | bytes 18874372
  41.0 4.6 %copy-start.1 = (bf16[384,128,128]{2,1,0:T(8,128)(2,1)S(1)}, bf16[384,128,128]{2,1,0:T(8,128)(2,1)}, u32[]{:S(2)}) copy-start(bf16[384,128,128]{2,1,0:T(8,128)(2,1)} %copy-done) | copy-start | bytes 37748740
  45.6 2.8 %copy-start.3 = (bf16[384,64,128]{2,1,0:T(8,128)(2,1)S(1)}, bf16[384,64,128]{2,1,0:T(8,128)(2,1)}, u32[]{:S(2)}) copy-start(bf16[384,64,128]{2,1,0:T(8,128)(2,1)} %copy-done.2) | copy-start | bytes 18874372
  53.7 18.5 %collective-permute-start = (bf16[2,64,512]{2,1,0:T(8,128)(2,1)S(1)}, bf16[2,64,512]{2,1,0:T(8,128)(2,1)S(1)}, u32[]{:S(2)}, u32[]{:S(2)}) collective-permute-start(bf16[2,64,512]{2,1,0:T(8,128)(2,1)S(1)} %get-tuple-element.16), channel_id=1, source_target_pairs={{0,4},{4,8},{8,12},{12,16},{16,20},{20,24},{24,28},{1,5},{5,9},{9,... | collective-permute-start | bytes 393224 | tf_op jit(solution)/shard_map/ppermute | solution.py:44
  55.7 16.5 %collective-permute-start.1 = (bf16[256,128]{1,0:T(8,128)(2,1)S(1)}, bf16[256,128]{1,0:T(8,128)(2,1)S(1)}, u32[]{:S(2)}, u32[]{:S(2)}) collective-permute-start(bf16[256,128]{1,0:T(8,128)(2,1)S(1)} %get-tuple-element.17), channel_id=1, source_target_pairs={{0,1},{1,2},{2,3},{4,5},{5,6},{6,7},{8,9},{9,10},{10,11},{12,13},{... | collective-permute-start | bytes 196616 | tf_op jit(solution)/shard_map/ppermute | solution.py:44
  61.2 11.0 %collective-permute-start.2 = (bf16[64,128]{1,0:T(8,128)(2,1)S(1)}, bf16[64,128]{1,0:T(8,128)(2,1)S(1)}, u32[]{:S(2)}, u32[]{:S(2)}) collective-permute-start(bf16[64,128]{1,0:T(8,128)(2,1)S(1)} %get-tuple-element.18), channel_id=1, source_target_pairs={{0,5},{1,6},{2,7},{4,9},{5,10},{6,11},{8,13},{9,14},{10,15},{12,17... | collective-permute-start | bytes 49160 | tf_op jit(solution)/shard_map/ppermute | solution.py:499

commit v2 on v1

--- a/solution.py
+++ b/solution.py
@@ -13,7 +13,8 @@
 TILE_V = 512
 QUAD = 4
 UNROLL = 4
-SPLIT = 1
+STEP = 2 * UNROLL
+RING = 4
 
 def _fit(fn, degree):
     span = math.pi ** 2
@@ -53,8 +54,8 @@
 
 
 def kernels_body(
-    list_hbm, depth_hbm, amp_hbm, phase_hbm, out_ref,
-    chosen_list, depth, amp, phase, table, screen, halves, made, small_sems, bulk_sems,
+    list_hbm, count_hbm, depth_hbm, amp_hbm, phase_hbm, out_ref,
+    chosen_list, count, depth, amp, phase, table, screen, halves, made, small_sems, bulk_sems,
 ):
     screens, size, _ = amp.shape
     planes = depth.shape[0]
@@ -62,6 +63,7 @@
     small = [
         pltpu.make_async_copy(depth_hbm, depth, small_sems.at[0]),
         pltpu.make_async_copy(list_hbm, chosen_list, small_sems.at[1]),
+        pltpu.make_async_copy(count_hbm, count, small_sems.at[2]),
     ]
     for copy in small:
         copy.start()
@@ -131,23 +133,23 @@
     @pl.loop(0, tiles)
     def _(t):
         for c in range(capacity):
-            which = chosen_list[c, t]
-            chosen = made[jnp.maximum(which, 0)]
-            out_ref[t * capacity + c] = jnp.where(which >= 0, chosen, jnp.zeros_like(chosen))
-
-
-def make_kernels(aperture_amp, aperture_phase, plane_depths, chosen_list, kernel_size):
+            chosen = made[chosen_list[c, t]]
+            out_ref[t * capacity + c] = jnp.where(c < count[0, t], chosen, jnp.zeros_like(chosen))
+
+
+def make_kernels(aperture_amp, aperture_phase, plane_depths, chosen_list, counts, kernel_size):
     screens, size, _ = aperture_amp.shape
     planes = plane_depths.shape[0]
     capacity, tiles = chosen_list.shape
     hbm = pl.BlockSpec(memory_space=pl.ANY)
     return pl.pallas_call(
         kernels_body,
-        in_specs=[hbm] * 4,
+        in_specs=[hbm] * 5,
         out_specs=pl.BlockSpec(memory_space=pltpu.VMEM),
         out_shape=jax.ShapeDtypeStruct((tiles * capacity, kernel_size, 2 * kernel_size), jnp.bfloat16),
         scratch_shapes=[
             pltpu.SMEM((capacity, tiles), jnp.int32),
+            pltpu.SMEM((1, tiles), jnp.int32),
             pltpu.SMEM((planes,), jnp.float32),
             pltpu.VMEM((screens, size, size), jnp.bfloat16),
             pltpu.VMEM((screens, size, size), jnp.bfloat16),
@@ -155,76 +157,53 @@
             pltpu.VMEM((2 * size, size), jnp.bfloat16),
             pltpu.VMEM((planes, kernel_size, 2 * size), jnp.bfloat16),
             pltpu.VMEM((screens * planes, kernel_size, 2 * kernel_size), jnp.bfloat16),
-            pltpu.SemaphoreType.DMA((2,)),
+            pltpu.SemaphoreType.DMA((3,)),
             pltpu.SemaphoreType.DMA((2, screens)),
         ],
         compiler_params=pltpu.CompilerParams(vmem_limit_bytes=32 * 2**20),
         name="make_kernels",
-    )(in_hbm(chosen_list), in_hbm(plane_depths), in_hbm(aperture_amp), in_hbm(aperture_phase))
+    )(*map(in_hbm, (chosen_list, counts, plane_depths, aperture_amp, aperture_phase)))
 
 
 class Layout:
     def __init__(self, blocks, anchors):
-        step = 2 * UNROLL
-        self.parts = SPLIT + 1
-        buckets = SPLIT * anchors
-        self.quads = (blocks + (QUAD - 1) * buckets) // QUAD + 1 + self.parts * (step - 1) + UNROLL
+        self.parts = 2
+        quads = (blocks + (QUAD - 1) * anchors) // QUAD + 1 + self.parts * (STEP - 1)
+        self.quads = (quads + STEP - 1) // STEP * STEP
         self.anchor = self.parts + 1
-        self.block = self.anchor + self.quads
-        self.slot = self.block + self.quads * QUAD
-        self.total = self.slot + self.quads * QUAD
+        self.slot = self.anchor + self.quads
+        self.total = self.slot + (self.quads + UNROLL) * QUAD
 
 
 def plan_body(
-    pos_ref, slot_ref, count_ref, half_ref, left_hbm, right_hbm, plan_ref, left_ref, right_ref,
-    tally, cursor, sems, *, row_slots, col_slots, half_slots,
+    pos_ref, slot_ref, count_ref, left_hbm, right_hbm, plan_ref, left_ref, right_ref,
+    tally, cursor, sems, *, layout, row_slots, col_slots,
 ):
-    copies = [
-        pltpu.make_async_copy(left_hbm, left_ref, sems.at[0]),
-        pltpu.make_async_copy(right_hbm, right_ref, sems.at[1]),
-    ]
-    for copy in copies:
-        copy.start()
     anchors = row_slots * col_slots
     border = row_slots + col_slots - 1
-    layout = Layout(pos_ref.shape[0], anchors)
-    step = 2 * UNROLL
-
-    @pl.loop(0, SPLIT * anchors)
-    def _(b):
-        tally[b] = 0
-
     live = count_ref[0]
 
-    def bucket_of(j):
-        q = pos_ref[j]
-        row = q // col_slots
-        col = q % col_slots
-        rank = jnp.where(
-            row == row_slots - 1,
-            col,
-            jnp.where(
-                col == col_slots - 1, col_slots + row, border + row * (col_slots - 1) + col
-            ),
-        )
-        if SPLIT == 1:
-            return rank
-        other = (slot_ref[j] // half_slots) != half_ref[0]
-        return rank + jnp.where(other, anchors, 0)
+    def copies(block, place):
+        return [
+            pltpu.make_async_copy(left_hbm.at[block], left_ref.at[place], sems.at[0]),
+            pltpu.make_async_copy(right_hbm.at[block], right_ref.at[place], sems.at[1]),
+        ]
+
+    def put(block, place, slot):
+        plan_ref[layout.slot + place] = slot
+        for copy in copies(block, place):
+            copy.start()
+
+    @pl.loop(0, anchors)
+    def _(q):
+        tally[q] = 0
 
     @pl.loop(0, live)
     def _(j):
-        b = bucket_of(j)
-        tally[b] = tally[b] + 1
-
-    def dead(quad):
-        plan_ref[layout.anchor + quad] = 0
-        for e in range(QUAD):
-            plan_ref[layout.block + quad * QUAD + e] = 0
-            plan_ref[layout.slot + quad * QUAD + e] = -1
-
-    def lay(b, quad):
-        rank = lax.rem(b, anchors)
+        q = pos_ref[j]
+        tally[q] = tally[q] + 1
+
+    def lay(rank, quad):
         inner = rank - border
         q = jnp.where(
             rank < col_slots,
@@ -235,9 +214,9 @@
                 (inner // (col_slots - 1)) * col_slots + lax.rem(inner, col_slots - 1),
             ),
         )
-        number = tally[b]
+        number = tally[q]
         quads = (number + QUAD - 1) // QUAD
-        cursor[b] = quad * QUAD
+        cursor[q] = quad * QUAD
 
         @pl.loop(0, quads)
         def _(i):
@@ -245,63 +224,66 @@
 
         @pl.loop(quad * QUAD + number, (quad + quads) * QUAD)
         def _(i):
-            plan_ref[layout.block + i] = 0
-            plan_ref[layout.slot + i] = -1
+            put(0, i, -1)
 
         return quad + quads
 
-    ends = [border, anchors] if SPLIT == 1 else [anchors, anchors + border, 2 * anchors]
     quad = 0
     begin = 0
     plan_ref[0] = 0
-    for part, end in enumerate(ends):
+    for part, end in enumerate([border, anchors]):
         quad = lax.fori_loop(begin, end, lay, quad)
         begin = end
-        full = ((quad + step - 1) // step) * step
-        pl.loop(quad, full)(dead)
+        full = ((quad + STEP - 1) // STEP) * STEP
+
+        @pl.loop(quad, full)
+        def _(i):
+            plan_ref[layout.anchor + i] = 0
+            for e in range(QUAD):
+                put(0, i * QUAD + e, -1)
+
         quad = full
         plan_ref[part + 1] = quad
-    pl.loop(quad, quad + UNROLL)(dead)
+
+    @pl.loop(quad * QUAD, (quad + UNROLL) * QUAD)
+    def _(i):
+        plan_ref[layout.slot + i] = -1
 
     @pl.loop(0, live)
     def _(j):
-        b = bucket_of(j)
-        at = cursor[b]
-        cursor[b] = at + 1
-        plan_ref[layout.block + at] = j
-        slot = slot_ref[j]
-        plan_ref[layout.slot + at] = slot if SPLIT == 1 else lax.rem(slot, half_slots)
-
-    for copy in copies:
-        copy.wait()
-
-
-def plan_blocks(block_pos, block_slot, block_count, half, vis_left, vis_right, half_slots):
+        q = pos_ref[j]
+        at = cursor[q]
+        cursor[q] = at + 1
+        put(j, at, slot_ref[j])
+
+    @pl.loop(0, quad * QUAD)
+    def _(i):
+        for copy in copies(0, 0):
+            copy.wait()
+
+
+def plan_blocks(block_pos, block_slot, block_count, vis_left, vis_right, layout):
     kernel_size = vis_right.shape[1]
     row_slots, col_slots = TILE_U // kernel_size, TILE_V // kernel_size
-    layout = Layout(block_pos.shape[0], row_slots * col_slots)
     smem = pl.BlockSpec(memory_space=pltpu.SMEM)
     hbm = pl.BlockSpec(memory_space=pl.ANY)
-    vmem = pl.BlockSpec(memory_space=pltpu.VMEM)
+    places = layout.quads * QUAD
     return pl.pallas_call(
-        functools.partial(
-            plan_body, row_slots=row_slots, col_slots=col_slots, half_slots=half_slots
-        ),
-        in_specs=[smem] * 4 + [hbm] * 2,
-        out_specs=[smem, vmem, vmem],
+        functools.partial(plan_body, layout=layout, row_slots=row_slots, col_slots=col_slots),
+        in_specs=[smem] * 3 + [hbm] * 2,
+        out_specs=[smem, hbm, hbm],
         out_shape=[
             jax.ShapeDtypeStruct((layout.total,), jnp.int32),
-            pltpu.VMEM(vis_left.shape, vis_left.dtype),
-            pltpu.VMEM(vis_right.shape, vis_right.dtype),
+            pltpu.HBM((places,) + vis_left.shape[1:], vis_left.dtype),
+            pltpu.HBM((places,) + vis_right.shape[1:], vis_right.dtype),
         ],
         scratch_shapes=[
-            pltpu.SMEM((SPLIT * row_slots * col_slots,), jnp.int32),
-            pltpu.SMEM((SPLIT * row_slots * col_slots,), jnp.int32),
+            pltpu.SMEM((row_slots * col_slots,), jnp.int32),
+            pltpu.SMEM((row_slots * col_slots,), jnp.int32),
             pltpu.SemaphoreType.DMA((2,)),
         ],
-        compiler_params=pltpu.CompilerParams(vmem_limit_bytes=2**20),
         name="plan_blocks",
-    )(block_pos, block_slot, block_count, half, in_hbm(vis_left), in_hbm(vis_right))
+    )(block_pos, block_slot, block_count, in_hbm(vis_left), in_hbm(vis_right))
 
 
 def strip(sums, row_slots, col_slots, kernel_size, plane, a, col):
@@ -317,7 +299,7 @@
 
 
 def grid_body(
-    plan_ref, kern_ref, left_ref, right_ref, *rest, part, first_part, halo, row_slots, col_slots
+    plan_ref, kern_ref, left_hbm, right_hbm, *rest, part, first_part, halo, layout, row_slots, col_slots
 ):
     if first_part:
         sums, *rest = rest
@@ -325,24 +307,47 @@
         before, sums, *rest = rest
     if halo:
         row_ref, col_ref, corner_ref, *rest = rest
-    mixed = rest
+    left_ring, right_ring, sems, *mixed = rest
     slots, kernel_size, _ = kern_ref.shape
-    blocks, patch, _ = left_ref.shape
-    anchors = sums.shape[0]
-    layout = Layout(blocks, anchors)
+    patch = left_hbm.shape[1]
+    chunk = STEP * QUAD
+    base = plan_ref[part] // STEP
+    number = plan_ref[part + 1] // STEP - base
+
+    def fetch(i):
+        source = pl.ds((base + i) * chunk, chunk)
+        ring = lax.rem(i, RING)
+        return [
+            pltpu.make_async_copy(left_hbm.at[source], left_ring.at[ring], sems.at[0, ring]),
+            pltpu.make_async_copy(right_hbm.at[source], right_ring.at[ring], sems.at[1, ring]),
+        ]
+
+    def start(i):
+        @pl.when(i < number)
+        def _():
+            for copy in fetch(i):
+                copy.start()
+
+    def wait(i):
+        @pl.when(i < number)
+        def _():
+            for copy in fetch(i):
+                copy.wait()
+
+    for i in range(RING):
+        start(i)
     if first_part:
 
-        @pl.loop(0, anchors)
+        @pl.loop(0, sums.shape[0])
         def _(q):
             sums[q] = jnp.zeros(sums.shape[1:], sums.dtype)
 
     zero = jnp.zeros((kernel_size, patch), jnp.bfloat16)
 
-    def first(quad, ref, u):
+    def first(i, ring, at, ref, u):
         for e in range(QUAD):
-            at = quad * QUAD + e
-            slot = plan_ref[layout.slot + at]
-            right = right_ref[plan_ref[layout.block + at]]
+            slot = plan_ref[layout.slot + ((base + i) * STEP + at) * QUAD + e]
+            right = right_ring[ring, at * QUAD + e]
             kern = kern_ref[jnp.maximum(slot, 0)]
             kern = jnp.where(slot >= 0, kern, jnp.zeros_like(kern))
             spread = jnp.concatenate(
@@ -355,24 +360,27 @@
             ref[u, low, :patch] = -out[:, patch:]
             ref[u, low, patch:] = out[:, :patch]
 
-    def second(quad, ref, u):
-        left = jnp.concatenate(
-            [left_ref[plan_ref[layout.block + quad * QUAD + e]] for e in range(QUAD)], axis=1
-        )
-        sums[plan_ref[layout.anchor + quad]] += jnp.dot(left, ref[u], preferred_element_type=jnp.float32)
-
-    begin = plan_ref[part]
-    end = plan_ref[part + 1]
+    def second(i, ring, at, ref, u):
+        left = jnp.concatenate([left_ring[ring, at * QUAD + e] for e in range(QUAD)], axis=1)
+        q = plan_ref[layout.anchor + (base + i) * STEP + at]
+        sums[q] += jnp.dot(left, ref[u], preferred_element_type=jnp.float32)
+
+    wait(0)
     for u in range(UNROLL):
-        first(begin + u, mixed[0], u)
-
-    @pl.loop(0, (end - begin) // (2 * UNROLL))
+        first(0, 0, u, mixed[0], u)
+
+    @pl.loop(0, number)
     def _(i):
-        for h in range(2):
-            quad = begin + (2 * i + h) * UNROLL
-            for u in range(UNROLL):
-                first(quad + UNROLL + u, mixed[1 - h], u)
-                second(quad + u, mixed[h], u)
+        here = lax.rem(i, RING)
+        there = lax.rem(i + 1, RING)
+        wait(i + 1)
+        for u in range(UNROLL):
+            first(i, here, UNROLL + u, mixed[1], u)
+            second(i, here, u, mixed[0], u)
+        for u in range(UNROLL):
+            first(i + 1, there, u, mixed[0], u)
+            second(i, here, UNROLL + u, mixed[1], u)
+        start(i + RING)
 
     if not halo:
         return
@@ -397,16 +405,19 @@
             corner_ref[...] = edge.astype(corner_ref.dtype)
 
 
-def grid_part(plan, part, kernels, left, right, sums, halo):
+def grid_part(plan, part, kernels, left, right, sums, halo, layout):
     kernel_size = kernels.shape[1]
     patch = left.shape[1]
     row_slots, col_slots = TILE_U // kernel_size, TILE_V // kernel_size
     smem = pl.BlockSpec(memory_space=pltpu.SMEM)
     vmem = pl.BlockSpec(memory_space=pltpu.VMEM)
+    hbm = pl.BlockSpec(memory_space=pl.ANY)
     first_part = sums is None
-    operands = [plan, in_vmem(kernels), in_vmem(left), in_vmem(right)]
+    operands = [plan, in_vmem(kernels), in_hbm(left), in_hbm(right)]
+    in_specs = [smem, vmem, hbm, hbm]
     if not first_part:
         operands.append(in_vmem(sums))
+        in_specs.append(vmem)
     out_shape = [pltpu.VMEM((row_slots * col_slots, patch, 2 * patch), jnp.float32)]
     if halo:
         out_shape += [
@@ -416,14 +427,25 @@
         ]
     return pl.pallas_call(
         functools.partial(
-            grid_body, part=part, first_part=first_part, halo=halo, row_slots=row_slots, col_slots=col_slots
+            grid_body,
+            part=part,
+            first_part=first_part,
+            halo=halo,
+            layout=layout,
+            row_slots=row_slots,
+            col_slots=col_slots,
         ),
-        in_specs=[smem] + [vmem] * (len(operands) - 1),
+        in_specs=in_specs,
         out_specs=[vmem] * len(out_shape),
         out_shape=out_shape,
         input_output_aliases={} if first_part else {4: 0},
-        scratch_shapes=[pltpu.VMEM((UNROLL, QUAD * 2 * kernel_size, 2 * patch), jnp.bfloat16)] * 2,
-        compiler_params=pltpu.CompilerParams(vmem_limit_bytes=12 * 2**20),
+        scratch_shapes=[
+            pltpu.VMEM((RING, STEP * QUAD) + left.shape[1:], left.dtype),
+            pltpu.VMEM((RING, STEP * QUAD) + right.shape[1:], right.dtype),
+            pltpu.SemaphoreType.DMA((2, RING)),
+        ]
+        + [pltpu.VMEM((UNROLL, QUAD * 2 * kernel_size, 2 * patch), jnp.bfloat16)] * 2,
+        compiler_params=pltpu.CompilerParams(vmem_limit_bytes=24 * 2**20),
         name="grid_part",
     )(*operands)
 
@@ -479,17 +501,15 @@
     kernel_size = vis_right.shape[1]
     tiles, capacity = send_list.shape[1:]
     both = ("tu", "tv")
-    used = jnp.arange(capacity, dtype=jnp.int32)[:, None] < send_count
-    chosen_list = jnp.where(used, send_list[0].T, -1)
-    outgoing = make_kernels(aperture_amp, aperture_phase, plane_depths, chosen_list, kernel_size)
+    outgoing = make_kernels(
+        aperture_amp, aperture_phase, plane_depths, send_list[0].T, send_count, kernel_size
+    )
     outgoing = outgoing.reshape((tiles, capacity) + outgoing.shape[1:])
     arrived = lax.all_to_all(outgoing, both, split_axis=0, concat_axis=0, tiled=True)
     received = arrived.reshape((-1,) + arrived.shape[2:])
-    half = jnp.zeros((1,), jnp.int32)
-    plan, left, right = plan_blocks(
-        block_pos, block_slot, block_count, half, vis_left, vis_right, tiles * capacity
-    )
-    sums, row, col, corner = grid_part(plan, 0, received, left, right, None, True)
+    layout = Layout(block_pos.shape[0], (TILE_U // kernel_size) * (TILE_V // kernel_size))
+    plan, left, right = plan_blocks(block_pos, block_slot, block_count, vis_left, vis_right, layout)
+    sums, row, col, corner = grid_part(plan, 0, received, left, right, None, True, layout)
     row = from_behind(row, "tu", 1)
     col = from_behind(col, "tv", 1)
     rows, cols = lax.axis_size("tu"), lax.axis_size("tv")
@@ -497,7 +517,7 @@
         (i * cols + j, (i + 1) * cols + j + 1) for i in range(rows - 1) for j in range(cols - 1)
     ]
     corner = lax.ppermute(corner, both, diagonal)
-    (sums,) = grid_part(plan, 1, received, left, right, sums, False)
+    (sums,) = grid_part(plan, 1, received, left, right, sums, False, layout)
     return merge_tile(sums, row, col, corner)
 
 

time: 73.6 us -> 716 us (9.73)
  the two profiles are of different devices: /device:TPU:19 before, /device:TPU:11 now
where the time goes in v2:
time: 716 us; the launch traced here: 714 us
  Pallas kernels  650 us (91%)
  starting transfers between devices  62.7 us (9%)
    pallas_call x1, Pallas kernels, plan_blocks(): pl.pallas_call(functools.partial(plan_body, layout=layout, row_slots=row_...  624 us
    ppermute x1, starting transfers between devices, shards(): corner = lax.ppermute(corner, both, diagonal)  52.6 us
    pallas_call x2, Pallas kernels, grid_part(): pl.pallas_call(functools.partial(grid_body, part=part, first_part=first_p...  15.1 us
  transfers between devices with their start and end apart: 4, of which 0 were waited for; matrix products, arithmetic and copies ran while one was open for 0% of the time, Pallas kernels for 89%

profile of v2, /device:TPU:11, one launch (start us, length us, event | category | flops | bytes accessed | tf_op | source)
XLA Modules:
  0.0 714.2 jit_solution(2513509105318745561)
XLA Ops:
  0.0 9.2 %make_kernels.1 = bf16[64,64,128]{2,1,0:T(8,128)(2,1)} custom-call(s32[2,32]{1,0:T(2,128)} %bitcast.7, s32[1,32]{1,0:T(1,128)} %count_hbm.1, f32[4]{0:T(128)} %depth_hbm.1, bf16[4,512,512]{2,1,0:T(8,128)(2,1)} %amp_hbm.1, bf16[4,512,512]{2,1,0:T(8,128)(2,1)} %phase_hbm.1), custom_call_target="tpu_custom_call" | custom-call | tf_op jit(solution)/shard_map/make_kernels/pallas_call | solution.py:145
  9.2 6.3 all-to-all-start
  16.2 624.5 %plan_blocks.1 = (s32[699]{0:T(1024)}, bf16[544,128,128]{2,1,0:T(8,128)(2,1)}, bf16[544,64,128]{2,1,0:T(8,128)(2,1)}) custom-call(s32[384]{0:T(512)} %pos_ref.1, s32[384]{0:T(512)} %slot_ref.1, s32[1]{0:T(128)S(6)} %copy.13.count_ref, bf16[384,128,128]{2,1,0:T(8,128)(2,1)} %left_hbm.1, bf16[384,64,128]{2,1,0:T(8,128)(2,1)} %right_hbm.1), custom_call_target="tpu_custom_call" | custom-call | tf_op jit(solution)/shard_map/plan_blocks/pallas_call | solution.py:271
  640.7 0.0 all-to-all-done
  640.7 0.0 copy-start
  640.7 0.7 copy-done
  641.4 6.5 grid_part.2
  647.8 1.9 collective-permute-start
  649.8 1.9 collective-permute-start.1
  651.7 52.6 %collective-permute-start.2 = (bf16[64,128]{1,0:T(8,128)(2,1)S(1)}, bf16[64,128]{1,0:T(8,128)(2,1)S(1)}, u32[]{:S(2)}, u32[]{:S(2)}) collective-permute-start(bf16[64,128]{1,0:T(8,128)(2,1)S(1)} %get-tuple-element.18), channel_id=1, source_target_pairs={{0,5},{1,6},{2,7},{4,9},{5,10},{6,11},{8,13},{9,14},{10,15},{12,17... | collective-permute-start | bytes 49160 | tf_op jit(solution)/shard_map/ppermute | solution.py:519
  704.2 8.6 %grid_part.3.sums = f32[32,128,256]{2,1,0:T(8,128)S(1)} custom-call(s32[699]{0:T(1024)S(1)} %copy-done, bf16[64,64,128]{2,1,0:T(8,128)(2,1)S(1)} %bitcast.6, bf16[544,128,128]{2,1,0:T(8,128)(2,1)} %get-tuple-element.13.left_hbm, bf16[544,64,128]{2,1,0:T(8,128)(2,1)} %get-tuple-element.14.right_hbm, ...), custom_call_target="tpu_custom_call", output_to_operand_aliasing={{}: (4, {})} | custom-call | tf_op jit(solution)/shard_map/grid_part/pallas_call | solution.py:428
  712.9 0.0 collective-permute-done.2.corner_ref
  712.9 0.0 collective-permute-done.1.col_ref
  712.9 0.0 collective-permute-done.row_ref
  712.9 1.3 merge_tile.1
Async XLA Ops:
  9.2 631.5 %all-to-all-start = ((bf16[32,2,64,128]{3,2,1,0:T(8,128)(2,1)}), bf16[32,2,64,128]{3,2,1,0:T(8,128)(2,1)S(1)}, u32[]{:S(2)}, u32[]{:S(2)}) async-start(bf16[32,2,64,128]{3,2,1,0:T(8,128)(2,1)} %bitcast.2), calls=%async_computation | async-start | bytes 2097152 | tf_op jit(solution)/shard_map/all_to_all | solution.py:508
  640.7 0.7 copy-start
  647.8 65.0 %collective-permute-start = (bf16[2,64,512]{2,1,0:T(8,128)(2,1)S(1)}, bf16[2,64,512]{2,1,0:T(8,128)(2,1)S(1)}, u32[]{:S(2)}, u32[]{:S(2)}) collective-permute-start(bf16[2,64,512]{2,1,0:T(8,128)(2,1)S(1)} %get-tuple-element.16), channel_id=1, source_target_pairs={{0,4},{4,8},{8,12},{12,16},{16,20},{20,24},{24,28},{1,5},{5,9},{9,... | collective-permute-start | bytes 393224 | tf_op jit(solution)/shard_map/ppermute | solution.py:45
  649.8 63.1 %collective-permute-start.1 = (bf16[256,128]{1,0:T(8,128)(2,1)S(1)}, bf16[256,128]{1,0:T(8,128)(2,1)S(1)}, u32[]{:S(2)}, u32[]{:S(2)}) collective-permute-start(bf16[256,128]{1,0:T(8,128)(2,1)S(1)} %get-tuple-element.17), channel_id=1, source_target_pairs={{0,1},{1,2},{2,3},{4,5},{5,6},{6,7},{8,9},{9,10},{10,11},{12,13},{... | collective-permute-start | bytes 196616 | tf_op jit(solution)/shard_map/ppermute | solution.py:45
  651.7 61.2 %collective-permute-start.2 = (bf16[64,128]{1,0:T(8,128)(2,1)S(1)}, bf16[64,128]{1,0:T(8,128)(2,1)S(1)}, u32[]{:S(2)}, u32[]{:S(2)}) collective-permute-start(bf16[64,128]{1,0:T(8,128)(2,1)S(1)} %get-tuple-element.18), channel_id=1, source_target_pairs={{0,5},{1,6},{2,7},{4,9},{5,10},{6,11},{8,13},{9,14},{10,15},{12,17... | collective-permute-start | bytes 49160 | tf_op jit(solution)/shard_map/ppermute | solution.py:519

commit v3 on v2

--- a/solution.py
+++ b/solution.py
@@ -14,7 +14,7 @@
 QUAD = 4
 UNROLL = 4
 STEP = 2 * UNROLL
-RING = 4
+RING = 3
 
 def _fit(fn, degree):
     span = math.pi ** 2
@@ -176,8 +176,8 @@
 
 
 def plan_body(
-    pos_ref, slot_ref, count_ref, left_hbm, right_hbm, plan_ref, left_ref, right_ref,
-    tally, cursor, sems, *, layout, row_slots, col_slots,
+    pos_ref, slot_ref, count_ref, left_hbm, right_hbm, plan_ref, left_out, right_out,
+    left_ref, right_ref, tally, cursor, sems, *, layout, row_slots, col_slots,
 ):
     anchors = row_slots * col_slots
     border = row_slots + col_slots - 1
@@ -259,6 +259,25 @@
     @pl.loop(0, quad * QUAD)
     def _(i):
         for copy in copies(0, 0):
+            copy.wait()
+
+    chunk = STEP * QUAD
+
+    def writes(i):
+        rows = pl.ds(i * chunk, chunk)
+        return [
+            pltpu.make_async_copy(left_ref.at[rows], left_out.at[rows], sems.at[2]),
+            pltpu.make_async_copy(right_ref.at[rows], right_out.at[rows], sems.at[3]),
+        ]
+
+    @pl.loop(0, quad // STEP)
+    def _(i):
+        for copy in writes(i):
+            copy.start()
+
+    @pl.loop(0, quad // STEP)
+    def _(i):
+        for copy in writes(i):
             copy.wait()
 
 
@@ -278,10 +297,13 @@
             pltpu.HBM((places,) + vis_right.shape[1:], vis_right.dtype),
         ],
         scratch_shapes=[
+            pltpu.VMEM((places,) + vis_left.shape[1:], vis_left.dtype),
+            pltpu.VMEM((places,) + vis_right.shape[1:], vis_right.dtype),
             pltpu.SMEM((row_slots * col_slots,), jnp.int32),
             pltpu.SMEM((row_slots * col_slots,), jnp.int32),
-            pltpu.SemaphoreType.DMA((2,)),
+            pltpu.SemaphoreType.DMA((4,)),
         ],
+        compiler_params=pltpu.CompilerParams(vmem_limit_bytes=36 * 2**20),
         name="plan_blocks",
     )(block_pos, block_slot, block_count, in_hbm(vis_left), in_hbm(vis_right))
 
@@ -301,21 +323,22 @@
 def grid_body(
     plan_ref, kern_ref, left_hbm, right_hbm, *rest, part, first_part, halo, layout, row_slots, col_slots
 ):
-    if first_part:
-        sums, *rest = rest
-    else:
-        before, sums, *rest = rest
+    if not first_part:
+        rest = rest[4:]
+    sums, left_ring, right_ring, ahead, *rest = rest
     if halo:
         row_ref, col_ref, corner_ref, *rest = rest
-    left_ring, right_ring, sems, *mixed = rest
+    behind_ref, sems = rest
+    mixed = (ahead, behind_ref)
     slots, kernel_size, _ = kern_ref.shape
     patch = left_hbm.shape[1]
     chunk = STEP * QUAD
-    base = plan_ref[part] // STEP
-    number = plan_ref[part + 1] // STEP - base
+    begin = plan_ref[part] // STEP
+    end = plan_ref[part + 1] // STEP
+    total = plan_ref[layout.parts] // STEP
 
     def fetch(i):
-        source = pl.ds((base + i) * chunk, chunk)
+        source = pl.ds(i * chunk, chunk)
         ring = lax.rem(i, RING)
         return [
             pltpu.make_async_copy(left_hbm.at[source], left_ring.at[ring], sems.at[0, ring]),
@@ -323,20 +346,19 @@
         ]
 
     def start(i):
-        @pl.when(i < number)
+        @pl.when(i < total)
         def _():
             for copy in fetch(i):
                 copy.start()
 
     def wait(i):
-        @pl.when(i < number)
+        @pl.when(i < total)
         def _():
             for copy in fetch(i):
                 copy.wait()
 
-    for i in range(RING):
-        start(i)
     if first_part:
+        start(0)
 
         @pl.loop(0, sums.shape[0])
         def _(q):
@@ -346,7 +368,7 @@
 
     def first(i, ring, at, ref, u):
         for e in range(QUAD):
-            slot = plan_ref[layout.slot + ((base + i) * STEP + at) * QUAD + e]
+            slot = plan_ref[layout.slot + (i * STEP + at) * QUAD + e]
             right = right_ring[ring, at * QUAD + e]
             kern = kern_ref[jnp.maximum(slot, 0)]
             kern = jnp.where(slot >= 0, kern, jnp.zeros_like(kern))
@@ -362,26 +384,33 @@
 
     def second(i, ring, at, ref, u):
         left = jnp.concatenate([left_ring[ring, at * QUAD + e] for e in range(QUAD)], axis=1)
-        q = plan_ref[layout.anchor + (base + i) * STEP + at]
+        q = plan_ref[layout.anchor + i * STEP + at]
         sums[q] += jnp.dot(left, ref[u], preferred_element_type=jnp.float32)
 
-    wait(0)
-    for u in range(UNROLL):
-        first(0, 0, u, mixed[0], u)
-
-    @pl.loop(0, number)
+    if first_part:
+        wait(0)
+        start(1)
+        for u in range(UNROLL):
+            first(0, 0, u, mixed[0], u)
+
+    @pl.loop(begin, end)
     def _(i):
         here = lax.rem(i, RING)
         there = lax.rem(i + 1, RING)
-        wait(i + 1)
+        start(i + 2)
+        if first_part:
+            wait(i + 1)
+        else:
+            pl.when(i > begin)(lambda: wait(i + 1))
         for u in range(UNROLL):
             first(i, here, UNROLL + u, mixed[1], u)
             second(i, here, u, mixed[0], u)
         for u in range(UNROLL):
             first(i + 1, there, u, mixed[0], u)
             second(i, here, UNROLL + u, mixed[1], u)
-        start(i + RING)
-
+
+    if first_part:
+        wait(end + 1)
     if not halo:
         return
     low = lax.broadcasted_iota(jnp.int32, (kernel_size, patch), 1) < kernel_size
@@ -405,27 +434,29 @@
             corner_ref[...] = edge.astype(corner_ref.dtype)
 
 
-def grid_part(plan, part, kernels, left, right, sums, halo, layout):
+def grid_part(plan, part, kernels, left, right, carried, halo, layout):
     kernel_size = kernels.shape[1]
     patch = left.shape[1]
     row_slots, col_slots = TILE_U // kernel_size, TILE_V // kernel_size
     smem = pl.BlockSpec(memory_space=pltpu.SMEM)
     vmem = pl.BlockSpec(memory_space=pltpu.VMEM)
     hbm = pl.BlockSpec(memory_space=pl.ANY)
-    first_part = sums is None
-    operands = [plan, in_vmem(kernels), in_hbm(left), in_hbm(right)]
-    in_specs = [smem, vmem, hbm, hbm]
-    if not first_part:
-        operands.append(in_vmem(sums))
-        in_specs.append(vmem)
-    out_shape = [pltpu.VMEM((row_slots * col_slots, patch, 2 * patch), jnp.float32)]
+    first_part = carried is None
+    carried = [] if first_part else [in_vmem(array) for array in carried]
+    mixed_shape = (UNROLL, QUAD * 2 * kernel_size, 2 * patch)
+    out_shape = [
+        pltpu.VMEM((row_slots * col_slots, patch, 2 * patch), jnp.float32),
+        pltpu.VMEM((RING, STEP * QUAD) + left.shape[1:], left.dtype),
+        pltpu.VMEM((RING, STEP * QUAD) + right.shape[1:], right.dtype),
+        pltpu.VMEM(mixed_shape, jnp.bfloat16),
+    ]
     if halo:
         out_shape += [
             jax.ShapeDtypeStruct((2, kernel_size, TILE_V), jnp.bfloat16),
             jax.ShapeDtypeStruct((TILE_U, 2 * kernel_size), jnp.bfloat16),
             jax.ShapeDtypeStruct((kernel_size, 2 * kernel_size), jnp.bfloat16),
         ]
-    return pl.pallas_call(
+    out = pl.pallas_call(
         functools.partial(
             grid_body,
             part=part,
@@ -435,19 +466,18 @@
             row_slots=row_slots,
             col_slots=col_slots,
         ),
-        in_specs=in_specs,
+        in_specs=[smem, vmem, hbm, hbm] + [vmem] * len(carried),
         out_specs=[vmem] * len(out_shape),
         out_shape=out_shape,
-        input_output_aliases={} if first_part else {4: 0},
+        input_output_aliases={4 + i: i for i in range(len(carried))},
         scratch_shapes=[
-            pltpu.VMEM((RING, STEP * QUAD) + left.shape[1:], left.dtype),
-            pltpu.VMEM((RING, STEP * QUAD) + right.shape[1:], right.dtype),
+            pltpu.VMEM(mixed_shape, jnp.bfloat16),
             pltpu.SemaphoreType.DMA((2, RING)),
-        ]
-        + [pltpu.VMEM((UNROLL, QUAD * 2 * kernel_size, 2 * patch), jnp.bfloat16)] * 2,
-        compiler_params=pltpu.CompilerParams(vmem_limit_bytes=24 * 2**20),
+        ],
+        compiler_params=pltpu.CompilerParams(vmem_limit_bytes=12 * 2**20),
         name="grid_part",
-    )(*operands)
+    )(plan, in_vmem(kernels), in_hbm(left), in_hbm(right), *carried)
+    return out[:4], out[4:]
 
 
 def merge_body(sums, row_ref, col_ref, corner_ref, out_ref):
@@ -509,7 +539,7 @@
     received = arrived.reshape((-1,) + arrived.shape[2:])
     layout = Layout(block_pos.shape[0], (TILE_U // kernel_size) * (TILE_V // kernel_size))
     plan, left, right = plan_blocks(block_pos, block_slot, block_count, vis_left, vis_right, layout)
-    sums, row, col, corner = grid_part(plan, 0, received, left, right, None, True, layout)
+    carried, (row, col, corner) = grid_part(plan, 0, received, left, right, None, True, layout)
     row = from_behind(row, "tu", 1)
     col = from_behind(col, "tv", 1)
     rows, cols = lax.axis_size("tu"), lax.axis_size("tv")
@@ -517,8 +547,8 @@
         (i * cols + j, (i + 1) * cols + j + 1) for i in range(rows - 1) for j in range(cols - 1)
     ]
     corner = lax.ppermute(corner, both, diagonal)
-    (sums,) = grid_part(plan, 1, received, left, right, sums, False, layout)
-    return merge_tile(sums, row, col, corner)
+    carried, _ = grid_part(plan, 1, received, left, right, carried, False, layout)
+    return merge_tile(carried[0], row, col, corner)
 
 
 def solution(mesh):

time: 716 us -> 71.1 us (0.10)
  the two profiles are of different devices: /device:TPU:11 before, /device:TPU:1 now
where the time goes in v3:
time: 71.1 us; the launch traced here: 71.6 us
  Pallas kernels  51.2 us (72%)
  starting transfers between devices  16.6 us (23%)
  waiting for transfers between devices  2.92 us (4%)
  between operations  0.75 us (1%)
    pallas_call x1, Pallas kernels, plan_blocks(): pl.pallas_call(functools.partial(plan_body, layout=layout, row_slots=row_...  21.7 us
    pallas_call x2, Pallas kernels, grid_part(): pl.pallas_call(functools.partial(grid_body, part=part, first_part=first_p...  19 us
    pallas_call x1, Pallas kernels, make_kernels(): pl.pallas_call(kernels_body, in_specs=[hbm] * 5, out_specs=pl.BlockSpec(m...  9.21 us
    ppermute x2, starting transfers between devices, from_behind(): return lax.ppermute(block, axis, route)  7.54 us
    all_to_all x1, starting transfers between devices, shards(): lax.all_to_all(outgoing, both, split_axis=0, concat_axis=0, tiled=True)  7.11 us
    all_to_all x1, waiting for transfers between devices, shards(): lax.all_to_all(outgoing, both, split_axis=0, concat_axis=0, tiled=True)  2.91 us
    ppermute x1, starting transfers between devices, shards(): corner = lax.ppermute(corner, both, diagonal)  1.99 us
  transfers between devices with their start and end apart: 4, of which 1 were waited for; matrix products, arithmetic and copies ran while one was open for 0% of the time, Pallas kernels for 45%

profile of v3, /device:TPU:1, one launch (start us, length us, event | category | flops | bytes accessed | tf_op | source)
XLA Modules:
  0.0 71.6 jit_solution(8493139283682545672)
XLA Ops:
  0.0 0.0 copy-start
  0.0 0.0 copy-start.1
  0.0 9.2 %make_kernels.1 = bf16[64,64,128]{2,1,0:T(8,128)(2,1)} custom-call(s32[2,32]{1,0:T(2,128)} %bitcast.7, s32[1,32]{1,0:T(1,128)} %count_hbm.1, f32[4]{0:T(128)} %depth_hbm.1, bf16[4,512,512]{2,1,0:T(8,128)(2,1)} %amp_hbm.1, bf16[4,512,512]{2,1,0:T(8,128)(2,1)} %phase_hbm.1), custom_call_target="tpu_custom_call" | custom-call | tf_op jit(solution)/shard_map/make_kernels/pallas_call | solution.py:145
  9.2 7.1 %all-to-all-start = ((bf16[32,2,64,128]{3,2,1,0:T(8,128)(2,1)}), bf16[32,2,64,128]{3,2,1,0:T(8,128)(2,1)S(1)}, u32[]{:S(2)}, u32[]{:S(2)}) async-start(bf16[32,2,64,128]{3,2,1,0:T(8,128)(2,1)} %bitcast.2), calls=%async_computation | async-start | bytes 2097152 | tf_op jit(solution)/shard_map/all_to_all | solution.py:538
  17.0 0.0 copy-done
  17.0 0.0 copy-done.1
  17.0 21.7 %plan_blocks.1 = (s32[699]{0:T(1024)S(1)}, bf16[544,128,128]{2,1,0:T(8,128)(2,1)}, bf16[544,64,128]{2,1,0:T(8,128)(2,1)}) custom-call(s32[384]{0:T(512)S(1)} %copy-done, s32[384]{0:T(512)S(1)} %copy-done.1, s32[1]{0:T(128)S(6)} %copy.19.count_ref, bf16[384,128,128]{2,1,0:T(8,128)(2,1)} %left_hbm.1, bf16[384,64,128]{2,1,0:T(8,128)(2,1)} %right_hbm.1), custom_call_target="tpu_custom_call" | custom-call | tf_op jit(solution)/shard_map/plan_blocks/pallas_call | solution.py:290
  38.8 2.9 %all-to-all-done = bf16[32,2,64,128]{3,2,1,0:T(8,128)(2,1)S(1)} async-done(((bf16[32,2,64,128]{3,2,1,0:T(8,128)(2,1)}), bf16[32,2,64,128]{3,2,1,0:T(8,128)(2,1)S(1)}, u32[]{:S(2)}, u32[]{:S(2)}) %all-to-all-start) | async-done | bytes 1048608 | tf_op jit(solution)/shard_map/all_to_all | solution.py:538
  41.7 8.8 %grid_part.2 = (f32[32,128,256]{2,1,0:T(8,128)S(1)}, bf16[3,32,128,128]{3,2,1,0:T(8,128)(2,1)S(1)}, bf16[3,32,64,128]{3,2,1,0:T(8,128)(2,1)S(1)}, bf16[4,512,256...) custom-call(s32[699]{0:T(1024)S(1)} %get-tuple-element.16.plan_ref, ...), custom_call_target="tpu_custom_call" | custom-call | tf_op jit(solution)/shard_map/grid_part/pallas_call | solution.py:459
  50.5 1.3 %collective-permute-start = (bf16[2,64,512]{2,1,0:T(8,128)(2,1)S(1)}, bf16[2,64,512]{2,1,0:T(8,128)(2,1)S(1)}, u32[]{:S(2)}, u32[]{:S(2)}) collective-permute-start(bf16[2,64,512]{2,1,0:T(8,128)(2,1)S(1)} %get-tuple-element.24), channel_id=1, source_target_pairs={{0,4},{4,8},{8,12},{12,16},{16,20},{20,24},{24,28},{1,5},{5,9},{9,... | collective-permute-start | bytes 393224 | tf_op jit(solution)/shard_map/ppermute | solution.py:45
  51.8 6.2 %collective-permute-start.1 = (bf16[256,128]{1,0:T(8,128)(2,1)S(1)}, bf16[256,128]{1,0:T(8,128)(2,1)S(1)}, u32[]{:S(2)}, u32[]{:S(2)}) collective-permute-start(bf16[256,128]{1,0:T(8,128)(2,1)S(1)} %get-tuple-element.25), channel_id=1, source_target_pairs={{0,1},{1,2},{2,3},{4,5},{5,6},{6,7},{8,9},{9,10},{10,11},{12,13},{... | collective-permute-start | bytes 196616 | tf_op jit(solution)/shard_map/ppermute | solution.py:45
  58.1 2.0 %collective-permute-start.2 = (bf16[64,128]{1,0:T(8,128)(2,1)S(1)}, bf16[64,128]{1,0:T(8,128)(2,1)S(1)}, u32[]{:S(2)}, u32[]{:S(2)}) collective-permute-start(bf16[64,128]{1,0:T(8,128)(2,1)S(1)} %get-tuple-element.26), channel_id=1, source_target_pairs={{0,5},{1,6},{2,7},{4,9},{5,10},{6,11},{8,13},{9,14},{10,15},{12,17... | collective-permute-start | bytes 49160 | tf_op jit(solution)/shard_map/ppermute | solution.py:549
  60.1 10.1 %grid_part.3 = (f32[32,128,256]{2,1,0:T(8,128)S(1)}, bf16[3,32,128,128]{3,2,1,0:T(8,128)(2,1)S(1)}, bf16[3,32,64,128]{3,2,1,0:T(8,128)(2,1)S(1)}, bf16[4,512,256]{2,1,0:T(8,128)(2,1)S(1)}) custom-call(s32[699]{0:T(1024)S(1)} %get-tuple-element.16.plan_ref, ...), custom_call_target="tpu_custom_call", output_to_operand_aliasing={{0}: (4, {}), {1}: (5, {}), {2}: (6, {}), {3}: (7, {})} | custom-call | tf_op jit(solution)/shard_map/grid_part/pallas_call | solution.py:459
  70.2 0.0 collective-permute-done.2.corner_ref
  70.2 0.0 collective-permute-done.1.col_ref
  70.2 0.0 collective-permute-done.row_ref
  70.2 1.3 %merge_tile.1 = f32[2,256,512]{2,1,0:T(8,128)} custom-call(f32[32,128,256]{2,1,0:T(8,128)S(1)} %get-tuple-element.23.sums, bf16[2,64,512]{2,1,0:T(8,128)(2,1)S(1)} %collective-permute-done.row_ref, bf16[256,128]{1,0:T(8,128)(2,1)S(1)} %collective-permute-done.1.col_ref, bf16[64,128]{1,0:T(8,128)(2,1)S(1)} %collective-permute-done.2.corner_ref), custom_call_target="tpu_custom_call" | custom-call | tf_op jit(solution)/shard_map/merge_tile/pallas_call | solution.py:509
Async XLA Ops:
  0.0 17.0 %copy-start = (s32[384]{0:T(512)S(1)}, s32[384]{0:T(512)}, u32[]{:S(2)}) copy-start(s32[384]{0:T(512)} %pos_ref.1) | copy-start | bytes 4612
  0.0 17.0 %copy-start.1 = (s32[384]{0:T(512)S(1)}, s32[384]{0:T(512)}, u32[]{:S(2)}) copy-start(s32[384]{0:T(512)} %slot_ref.1) | copy-start | bytes 4612
  9.2 32.4 %all-to-all-start = ((bf16[32,2,64,128]{3,2,1,0:T(8,128)(2,1)}), bf16[32,2,64,128]{3,2,1,0:T(8,128)(2,1)S(1)}, u32[]{:S(2)}, u32[]{:S(2)}) async-start(bf16[32,2,64,128]{3,2,1,0:T(8,128)(2,1)} %bitcast.2), calls=%async_computation | async-start | bytes 2097152 | tf_op jit(solution)/shard_map/all_to_all | solution.py:538
  50.5 19.7 %collective-permute-start = (bf16[2,64,512]{2,1,0:T(8,128)(2,1)S(1)}, bf16[2,64,512]{2,1,0:T(8,128)(2,1)S(1)}, u32[]{:S(2)}, u32[]{:S(2)}) collective-permute-start(bf16[2,64,512]{2,1,0:T(8,128)(2,1)S(1)} %get-tuple-element.24), channel_id=1, source_target_pairs={{0,4},{4,8},{8,12},{12,16},{16,20},{20,24},{24,28},{1,5},{5,9},{9,... | collective-permute-start | bytes 393224 | tf_op jit(solution)/shard_map/ppermute | solution.py:45
  51.8 18.4 %collective-permute-start.1 = (bf16[256,128]{1,0:T(8,128)(2,1)S(1)}, bf16[256,128]{1,0:T(8,128)(2,1)S(1)}, u32[]{:S(2)}, u32[]{:S(2)}) collective-permute-start(bf16[256,128]{1,0:T(8,128)(2,1)S(1)} %get-tuple-element.25), channel_id=1, source_target_pairs={{0,1},{1,2},{2,3},{4,5},{5,6},{6,7},{8,9},{9,10},{10,11},{12,13},{... | collective-permute-start | bytes 196616 | tf_op jit(solution)/shard_map/ppermute | solution.py:45
  58.1 12.1 %collective-permute-start.2 = (bf16[64,128]{1,0:T(8,128)(2,1)S(1)}, bf16[64,128]{1,0:T(8,128)(2,1)S(1)}, u32[]{:S(2)}, u32[]{:S(2)}) collective-permute-start(bf16[64,128]{1,0:T(8,128)(2,1)S(1)} %get-tuple-element.26), channel_id=1, source_target_pairs={{0,5},{1,6},{2,7},{4,9},{5,10},{6,11},{8,13},{9,14},{10,15},{12,17... | collective-permute-start | bytes 49160 | tf_op jit(solution)/shard_map/ppermute | solution.py:549

commit v4 on v3

--- a/solution.py
+++ b/solution.py
@@ -14,7 +14,7 @@
 QUAD = 4
 UNROLL = 4
 STEP = 2 * UNROLL
-RING = 3
+RING = 4
 
 def _fit(fn, degree):
     span = math.pi ** 2
@@ -100,33 +100,30 @@
         table[low, :size] = imag_g
         table[low, size:] = real_g
 
-    width = 256
-
     @pl.loop(0, screens)
     def _(s):
         for copy in bulk(s):
             copy.wait()
-        for start in range(0, size, width):
-            cols = slice(start, start + width)
-            magnitude = amp[s, :, cols].astype(jnp.float32)
-            real_e, imag_e = cos_sin(phase[s, :, cols].astype(jnp.float32))
-            screen[:size, cols] = (magnitude * real_e).astype(jnp.bfloat16)
-            screen[size:, cols] = (magnitude * imag_e).astype(jnp.bfloat16)
-            product = jnp.dot(table[...], screen[:, cols], preferred_element_type=jnp.float32)
-            for p in range(planes):
-                base = p * 2 * kernel_size
-                halves[p, :, start : start + width] = product[base : base + kernel_size].astype(jnp.bfloat16)
-                halves[p, :, size + start : size + start + width] = product[
-                    base + kernel_size : base + 2 * kernel_size
-                ].astype(jnp.bfloat16)
+        magnitude = amp[s].astype(jnp.float32)
+        real_e, imag_e = cos_sin(phase[s].astype(jnp.float32))
+        screen[:size, :] = (magnitude * real_e).astype(jnp.bfloat16)
+        screen[size:, :] = (magnitude * imag_e).astype(jnp.bfloat16)
+        product = jnp.dot(table[...], screen[...], preferred_element_type=jnp.float32).astype(jnp.bfloat16)
         for p in range(planes):
-            second = lax.dot_general(
-                halves[p],
-                table[p * 2 * kernel_size : (p + 1) * 2 * kernel_size, :],
-                (((1,), (1,)), ((), ())),
-                preferred_element_type=jnp.float32,
-            )
-            made[s * planes + p] = (second * (1.0 / size)).astype(jnp.bfloat16)
+            base = p * 2 * kernel_size
+            halves[s, p, :, :size] = product[base : base + kernel_size]
+            halves[s, p, :, size:] = product[base + kernel_size : base + 2 * kernel_size]
+
+    for p in range(planes):
+        second = lax.dot_general(
+            jnp.concatenate([halves[s, p] for s in range(screens)], axis=0),
+            table[p * 2 * kernel_size : (p + 1) * 2 * kernel_size, :],
+            (((1,), (1,)), ((), ())),
+            preferred_element_type=jnp.float32,
+        )
+        second = (second * (1.0 / size)).astype(jnp.bfloat16)
+        for s in range(screens):
+            made[s * planes + p] = second[s * kernel_size : (s + 1) * kernel_size]
 
     capacity, tiles = chosen_list.shape
 
@@ -146,7 +143,7 @@
         kernels_body,
         in_specs=[hbm] * 5,
         out_specs=pl.BlockSpec(memory_space=pltpu.VMEM),
-        out_shape=jax.ShapeDtypeStruct((tiles * capacity, kernel_size, 2 * kernel_size), jnp.bfloat16),
+        out_shape=pltpu.VMEM((tiles * capacity, kernel_size, 2 * kernel_size), jnp.bfloat16),
         scratch_shapes=[
             pltpu.SMEM((capacity, tiles), jnp.int32),
             pltpu.SMEM((1, tiles), jnp.int32),
@@ -155,7 +152,7 @@
             pltpu.VMEM((screens, size, size), jnp.bfloat16),
             pltpu.VMEM((planes * 2 * kernel_size, 2 * size), jnp.bfloat16),
             pltpu.VMEM((2 * size, size), jnp.bfloat16),
-            pltpu.VMEM((planes, kernel_size, 2 * size), jnp.bfloat16),
+            pltpu.VMEM((screens, planes, kernel_size, 2 * size), jnp.bfloat16),
             pltpu.VMEM((screens * planes, kernel_size, 2 * kernel_size), jnp.bfloat16),
             pltpu.SemaphoreType.DMA((3,)),
             pltpu.SemaphoreType.DMA((2, screens)),
@@ -390,6 +387,7 @@
     if first_part:
         wait(0)
         start(1)
+        start(2)
         for u in range(UNROLL):
             first(0, 0, u, mixed[0], u)
 
@@ -397,11 +395,11 @@
     def _(i):
         here = lax.rem(i, RING)
         there = lax.rem(i + 1, RING)
-        start(i + 2)
+        start(i + 3)
         if first_part:
             wait(i + 1)
         else:
-            pl.when(i > begin)(lambda: wait(i + 1))
+            pl.when(i > begin + 1)(lambda: wait(i + 1))
         for u in range(UNROLL):
             first(i, here, UNROLL + u, mixed[1], u)
             second(i, here, u, mixed[0], u)
@@ -411,6 +409,7 @@
 
     if first_part:
         wait(end + 1)
+        wait(end + 2)
     if not halo:
         return
     low = lax.broadcasted_iota(jnp.int32, (kernel_size, patch), 1) < kernel_size

time: 71.1 us -> 66.4 us (0.934)
  the two profiles are of different devices: /device:TPU:1 before, /device:TPU:9 now
where the time goes in v4:
time: 66.4 us; the launch traced here: 66.2 us
  Pallas kernels  48 us (72%)
  starting transfers between devices  14.9 us (22%)
  waiting for transfers between devices  2.51 us (4%)
  between operations  0.75 us (1%)
    pallas_call x1, Pallas kernels, plan_blocks(): pl.pallas_call(functools.partial(plan_body, layout=layout, row_slots=row_...  22.1 us
    pallas_call x2, Pallas kernels, grid_part(): pl.pallas_call(functools.partial(grid_body, part=part, first_part=first_p...  15.8 us
    pallas_call x1, Pallas kernels, make_kernels(): pl.pallas_call(kernels_body, in_specs=[hbm] * 5, out_specs=pl.BlockSpec(m...  8.73 us
    all_to_all x1, starting transfers between devices, shards(): lax.all_to_all(outgoing, both, split_axis=0, concat_axis=0, tiled=True)  6.37 us
    ppermute x1, starting transfers between devices, shards(): corner = lax.ppermute(corner, both, diagonal)  4.72 us
    ppermute x2, starting transfers between devices, from_behind(): return lax.ppermute(block, axis, route)  3.84 us
    all_to_all x1, waiting for transfers between devices, shards(): lax.all_to_all(outgoing, both, split_axis=0, concat_axis=0, tiled=True)  2.5 us
    pallas_call x1, Pallas kernels, merge_tile(): pl.pallas_call(merge_body, in_specs=[vmem] * 4, out_specs=vmem, out_shape...  1.33 us
  transfers between devices with their start and end apart: 4, of which 1 were waited for; matrix products, arithmetic and copies ran while one was open for 0% of the time, Pallas kernels for 45%

profile of v4, /device:TPU:9, one launch (start us, length us, event | category | flops | bytes accessed | tf_op | source)
XLA Modules:
  0.0 66.2 jit_solution(2033532399307686727)
XLA Ops:
  0.0 0.0 copy-start
  0.0 0.0 copy-start.1
  0.0 8.7 %make_kernels.1 = bf16[64,64,128]{2,1,0:T(8,128)(2,1)} custom-call(s32[2,32]{1,0:T(2,128)} %bitcast.7, s32[1,32]{1,0:T(1,128)} %count_hbm.1, f32[4]{0:T(128)} %depth_hbm.1, bf16[4,512,512]{2,1,0:T(8,128)(2,1)} %amp_hbm.1, bf16[4,512,512]{2,1,0:T(8,128)(2,1)} %phase_hbm.1), custom_call_target="tpu_custom_call" | custom-call | tf_op jit(solution)/shard_map/make_kernels/pallas_call | solution.py:142
  8.7 6.4 %all-to-all-start = ((bf16[32,2,64,128]{3,2,1,0:T(8,128)(2,1)}), bf16[32,2,64,128]{3,2,1,0:T(8,128)(2,1)S(1)}, u32[]{:S(2)}, u32[]{:S(2)}) async-start(bf16[32,2,64,128]{3,2,1,0:T(8,128)(2,1)} %bitcast.2), calls=%async_computation | async-start | bytes 2097152 | tf_op jit(solution)/shard_map/all_to_all | solution.py:537
  15.8 0.0 copy-done
  15.8 0.0 copy-done.1
  15.8 22.1 %plan_blocks.1 = (s32[699]{0:T(1024)S(1)}, bf16[544,128,128]{2,1,0:T(8,128)(2,1)}, bf16[544,64,128]{2,1,0:T(8,128)(2,1)}) custom-call(s32[384]{0:T(512)S(1)} %copy-done, s32[384]{0:T(512)S(1)} %copy-done.1, s32[1]{0:T(128)S(6)} %copy.19.count_ref, bf16[384,128,128]{2,1,0:T(8,128)(2,1)} %left_hbm.1, bf16[384,64,128]{2,1,0:T(8,128)(2,1)} %right_hbm.1), custom_call_target="tpu_custom_call" | custom-call | tf_op jit(solution)/shard_map/plan_blocks/pallas_call | solution.py:287
  37.9 2.5 %all-to-all-done = bf16[32,2,64,128]{3,2,1,0:T(8,128)(2,1)S(1)} async-done(((bf16[32,2,64,128]{3,2,1,0:T(8,128)(2,1)}), bf16[32,2,64,128]{3,2,1,0:T(8,128)(2,1)S(1)}, u32[]{:S(2)}, u32[]{:S(2)}) %all-to-all-start) | async-done | bytes 1048608 | tf_op jit(solution)/shard_map/all_to_all | solution.py:537
  40.4 8.1 %grid_part.2 = (f32[32,128,256]{2,1,0:T(8,128)S(1)}, bf16[4,32,128,128]{3,2,1,0:T(8,128)(2,1)S(1)}, bf16[4,32,64,128]{3,2,1,0:T(8,128)(2,1)S(1)}, bf16[4,512,256...) custom-call(s32[699]{0:T(1024)S(1)} %get-tuple-element.16.plan_ref, ...), custom_call_target="tpu_custom_call" | custom-call | tf_op jit(solution)/shard_map/grid_part/pallas_call | solution.py:458
  48.5 1.9 %collective-permute-start = (bf16[2,64,512]{2,1,0:T(8,128)(2,1)S(1)}, bf16[2,64,512]{2,1,0:T(8,128)(2,1)S(1)}, u32[]{:S(2)}, u32[]{:S(2)}) collective-permute-start(bf16[2,64,512]{2,1,0:T(8,128)(2,1)S(1)} %get-tuple-element.24), channel_id=1, source_target_pairs={{0,4},{4,8},{8,12},{12,16},{16,20},{20,24},{24,28},{1,5},{5,9},{9,... | collective-permute-start | bytes 393224 | tf_op jit(solution)/shard_map/ppermute | solution.py:45
  50.4 1.9 %collective-permute-start.1 = (bf16[256,128]{1,0:T(8,128)(2,1)S(1)}, bf16[256,128]{1,0:T(8,128)(2,1)S(1)}, u32[]{:S(2)}, u32[]{:S(2)}) collective-permute-start(bf16[256,128]{1,0:T(8,128)(2,1)S(1)} %get-tuple-element.25), channel_id=1, source_target_pairs={{0,1},{1,2},{2,3},{4,5},{5,6},{6,7},{8,9},{9,10},{10,11},{12,13},{... | collective-permute-start | bytes 196616 | tf_op jit(solution)/shard_map/ppermute | solution.py:45
  52.4 4.7 %collective-permute-start.2 = (bf16[64,128]{1,0:T(8,128)(2,1)S(1)}, bf16[64,128]{1,0:T(8,128)(2,1)S(1)}, u32[]{:S(2)}, u32[]{:S(2)}) collective-permute-start(bf16[64,128]{1,0:T(8,128)(2,1)S(1)} %get-tuple-element.26), channel_id=1, source_target_pairs={{0,5},{1,6},{2,7},{4,9},{5,10},{6,11},{8,13},{9,14},{10,15},{12,17... | collective-permute-start | bytes 49160 | tf_op jit(solution)/shard_map/ppermute | solution.py:548
  57.1 7.7 %grid_part.3 = (f32[32,128,256]{2,1,0:T(8,128)S(1)}, bf16[4,32,128,128]{3,2,1,0:T(8,128)(2,1)S(1)}, bf16[4,32,64,128]{3,2,1,0:T(8,128)(2,1)S(1)}, bf16[4,512,256]{2,1,0:T(8,128)(2,1)S(1)}) custom-call(s32[699]{0:T(1024)S(1)} %get-tuple-element.16.plan_ref, ...), custom_call_target="tpu_custom_call", output_to_operand_aliasing={{0}: (4, {}), {1}: (5, {}), {2}: (6, {}), {3}: (7, {})} | custom-call | tf_op jit(solution)/shard_map/grid_part/pallas_call | solution.py:458
  64.8 0.0 collective-permute-done.2.corner_ref
  64.8 0.0 collective-permute-done.1.col_ref
  64.8 0.0 collective-permute-done.row_ref
  64.8 1.3 %merge_tile.1 = f32[2,256,512]{2,1,0:T(8,128)} custom-call(f32[32,128,256]{2,1,0:T(8,128)S(1)} %get-tuple-element.23.sums, bf16[2,64,512]{2,1,0:T(8,128)(2,1)S(1)} %collective-permute-done.row_ref, bf16[256,128]{1,0:T(8,128)(2,1)S(1)} %collective-permute-done.1.col_ref, bf16[64,128]{1,0:T(8,128)(2,1)S(1)} %collective-permute-done.2.corner_ref), custom_call_target="tpu_custom_call" | custom-call | tf_op jit(solution)/shard_map/merge_tile/pallas_call | solution.py:508
Async XLA Ops:
  0.0 15.8 %copy-start = (s32[384]{0:T(512)S(1)}, s32[384]{0:T(512)}, u32[]{:S(2)}) copy-start(s32[384]{0:T(512)} %pos_ref.1) | copy-start | bytes 4612
  0.0 15.8 %copy-start.1 = (s32[384]{0:T(512)S(1)}, s32[384]{0:T(512)}, u32[]{:S(2)}) copy-start(s32[384]{0:T(512)} %slot_ref.1) | copy-start | bytes 4612
  8.7 31.6 %all-to-all-start = ((bf16[32,2,64,128]{3,2,1,0:T(8,128)(2,1)}), bf16[32,2,64,128]{3,2,1,0:T(8,128)(2,1)S(1)}, u32[]{:S(2)}, u32[]{:S(2)}) async-start(bf16[32,2,64,128]{3,2,1,0:T(8,128)(2,1)} %bitcast.2), calls=%async_computation | async-start | bytes 2097152 | tf_op jit(solution)/shard_map/all_to_all | solution.py:537
  48.5 16.3 %collective-permute-start = (bf16[2,64,512]{2,1,0:T(8,128)(2,1)S(1)}, bf16[2,64,512]{2,1,0:T(8,128)(2,1)S(1)}, u32[]{:S(2)}, u32[]{:S(2)}) collective-permute-start(bf16[2,64,512]{2,1,0:T(8,128)(2,1)S(1)} %get-tuple-element.24), channel_id=1, source_target_pairs={{0,4},{4,8},{8,12},{12,16},{16,20},{20,24},{24,28},{1,5},{5,9},{9,... | collective-permute-start | bytes 393224 | tf_op jit(solution)/shard_map/ppermute | solution.py:45
  50.4 14.4 %collective-permute-start.1 = (bf16[256,128]{1,0:T(8,128)(2,1)S(1)}, bf16[256,128]{1,0:T(8,128)(2,1)S(1)}, u32[]{:S(2)}, u32[]{:S(2)}) collective-permute-start(bf16[256,128]{1,0:T(8,128)(2,1)S(1)} %get-tuple-element.25), channel_id=1, source_target_pairs={{0,1},{1,2},{2,3},{4,5},{5,6},{6,7},{8,9},{9,10},{10,11},{12,13},{... | collective-permute-start | bytes 196616 | tf_op jit(solution)/shard_map/ppermute | solution.py:45
  52.4 12.4 %collective-permute-start.2 = (bf16[64,128]{1,0:T(8,128)(2,1)S(1)}, bf16[64,128]{1,0:T(8,128)(2,1)S(1)}, u32[]{:S(2)}, u32[]{:S(2)}) collective-permute-start(bf16[64,128]{1,0:T(8,128)(2,1)S(1)} %get-tuple-element.26), channel_id=1, source_target_pairs={{0,5},{1,6},{2,7},{4,9},{5,10},{6,11},{8,13},{9,14},{10,15},{12,17... | collective-permute-start | bytes 49160 | tf_op jit(solution)/shard_map/ppermute | solution.py:548

commit v5 on v4

--- a/solution.py
+++ b/solution.py
@@ -51,6 +51,10 @@
 
 def in_vmem(array):
     return pltpu.with_memory_space_constraint(array, pltpu.VMEM)
+
+
+def in_smem(array):
+    return pltpu.with_memory_space_constraint(array, pltpu.SMEM)
 
 
 def kernels_body(
@@ -164,7 +168,7 @@
 
 class Layout:
     def __init__(self, blocks, anchors):
-        self.parts = 2
+        self.parts = 3
         quads = (blocks + (QUAD - 1) * anchors) // QUAD + 1 + self.parts * (STEP - 1)
         self.quads = (quads + STEP - 1) // STEP * STEP
         self.anchor = self.parts + 1
@@ -203,11 +207,11 @@
     def lay(rank, quad):
         inner = rank - border
         q = jnp.where(
-            rank < col_slots,
-            (row_slots - 1) * col_slots + rank,
+            rank < row_slots,
+            rank * col_slots + col_slots - 1,
             jnp.where(
                 rank < border,
-                (rank - col_slots) * col_slots + col_slots - 1,
+                (row_slots - 1) * col_slots + rank - row_slots,
                 (inner // (col_slots - 1)) * col_slots + lax.rem(inner, col_slots - 1),
             ),
         )
@@ -228,7 +232,7 @@
     quad = 0
     begin = 0
     plan_ref[0] = 0
-    for part, end in enumerate([border, anchors]):
+    for part, end in enumerate([row_slots, border, anchors]):
         quad = lax.fori_loop(begin, end, lay, quad)
         begin = end
         full = ((quad + STEP - 1) // STEP) * STEP
@@ -253,12 +257,13 @@
         cursor[q] = at + 1
         put(j, at, slot_ref[j])
 
-    @pl.loop(0, quad * QUAD)
+    chunk = STEP * QUAD
+
+    @pl.loop(0, quad // STEP)
     def _(i):
-        for copy in copies(0, 0):
-            copy.wait()
-
-    chunk = STEP * QUAD
+        rows = pl.ds(0, chunk)
+        pltpu.make_async_copy(left_hbm.at[rows], left_ref.at[rows], sems.at[0]).wait()
+        pltpu.make_async_copy(right_hbm.at[rows], right_ref.at[rows], sems.at[1]).wait()
 
     def writes(i):
         rows = pl.ds(i * chunk, chunk)
@@ -289,7 +294,7 @@
         in_specs=[smem] * 3 + [hbm] * 2,
         out_specs=[smem, hbm, hbm],
         out_shape=[
-            jax.ShapeDtypeStruct((layout.total,), jnp.int32),
+            pltpu.SMEM((layout.total,), jnp.int32),
             pltpu.HBM((places,) + vis_left.shape[1:], vis_left.dtype),
             pltpu.HBM((places,) + vis_right.shape[1:], vis_right.dtype),
         ],
@@ -318,13 +323,13 @@
 
 
 def grid_body(
-    plan_ref, kern_ref, left_hbm, right_hbm, *rest, part, first_part, halo, layout, row_slots, col_slots
+    plan_ref, kern_ref, left_hbm, right_hbm, *rest, part, first_part, layout, row_slots, col_slots
 ):
     if not first_part:
         rest = rest[4:]
     sums, left_ring, right_ring, ahead, *rest = rest
-    if halo:
-        row_ref, col_ref, corner_ref, *rest = rest
+    if first_part:
+        col_ref, *rest = rest
     behind_ref, sems = rest
     mixed = (ahead, behind_ref)
     slots, kernel_size, _ = kern_ref.shape
@@ -347,6 +352,12 @@
         def _():
             for copy in fetch(i):
                 copy.start()
+
+    def wait_new(i):
+        if first_part:
+            wait(i)
+        else:
+            pl.when(i > begin + 2)(lambda: wait(i))
 
     def wait(i):
         @pl.when(i < total)
@@ -396,10 +407,7 @@
         here = lax.rem(i, RING)
         there = lax.rem(i + 1, RING)
         start(i + 3)
-        if first_part:
-            wait(i + 1)
-        else:
-            pl.when(i > begin + 1)(lambda: wait(i + 1))
+        wait_new(i + 1)
         for u in range(UNROLL):
             first(i, here, UNROLL + u, mixed[1], u)
             second(i, here, u, mixed[0], u)
@@ -407,33 +415,50 @@
             first(i + 1, there, u, mixed[0], u)
             second(i, here, UNROLL + u, mixed[1], u)
 
-    if first_part:
-        wait(end + 1)
-        wait(end + 2)
-    if not halo:
+    wait_new(end + 1)
+    wait_new(end + 2)
+    if not first_part:
         return
     low = lax.broadcasted_iota(jnp.int32, (kernel_size, patch), 1) < kernel_size
     take = functools.partial(strip, sums, row_slots, col_slots, kernel_size)
-    for plane in range(2):
-        behind = 0.0
-        for tile in range(col_slots // 2):
-            even = take(plane, row_slots, 2 * tile)
-            odd = pltpu.roll(take(plane, row_slots, 2 * tile + 1), kernel_size, 1)
-            row_ref[plane, :, tile * patch : (tile + 1) * patch] = (
-                even + jnp.where(low, behind, odd)
-            ).astype(row_ref.dtype)
-            behind = odd
     for a in range(row_slots + 1):
         real = pltpu.roll(take(0, a, col_slots - 1), kernel_size, 1)
-        imag = take(1, a, col_slots - 1)
-        edge = jnp.where(low, real, imag)
-        if a < row_slots:
-            col_ref[a * kernel_size : (a + 1) * kernel_size, :] = edge.astype(col_ref.dtype)
-        else:
-            corner_ref[...] = edge.astype(corner_ref.dtype)
-
-
-def grid_part(plan, part, kernels, left, right, carried, halo, layout):
+        edge = jnp.where(low, real, take(1, a, col_slots - 1))
+        col_ref[a * kernel_size : (a + 1) * kernel_size, :] = edge.astype(col_ref.dtype)
+
+
+def row_body(before, col_ref, sums, row_ref, *, row_slots, col_slots):
+    kernel_size = row_ref.shape[1]
+    patch = sums.shape[1]
+    low = lax.broadcasted_iota(jnp.int32, (kernel_size, patch), 1) < kernel_size
+    take = functools.partial(strip, sums, row_slots, col_slots, kernel_size)
+    corner = col_ref[row_slots * kernel_size :, :].astype(jnp.float32)
+    for plane in range(2):
+        behind = corner if plane == 0 else pltpu.roll(corner, kernel_size, 1)
+        for tile in range(col_slots // 2):
+            odd = pltpu.roll(take(plane, row_slots, 2 * tile + 1), kernel_size, 1)
+            value = take(plane, row_slots, 2 * tile) + jnp.where(low, behind, odd)
+            row_ref[plane, :, tile * patch : (tile + 1) * patch] = value.astype(row_ref.dtype)
+            behind = odd
+
+
+def row_halo(sums, col, kernel_size):
+    vmem = pl.BlockSpec(memory_space=pltpu.VMEM)
+    return pl.pallas_call(
+        functools.partial(row_body, row_slots=TILE_U // kernel_size, col_slots=TILE_V // kernel_size),
+        in_specs=[vmem] * 2,
+        out_specs=[vmem] * 2,
+        out_shape=[
+            pltpu.VMEM(sums.shape, sums.dtype),
+            pltpu.VMEM((2, kernel_size, TILE_V), jnp.bfloat16),
+        ],
+        input_output_aliases={0: 0},
+        compiler_params=pltpu.CompilerParams(vmem_limit_bytes=4 * 2**20),
+        name="row_halo",
+    )(in_vmem(sums), in_vmem(col))
+
+
+def grid_part(plan, part, kernels, left, right, carried, layout):
     kernel_size = kernels.shape[1]
     patch = left.shape[1]
     row_slots, col_slots = TILE_U // kernel_size, TILE_V // kernel_size
@@ -449,18 +474,13 @@
         pltpu.VMEM((RING, STEP * QUAD) + right.shape[1:], right.dtype),
         pltpu.VMEM(mixed_shape, jnp.bfloat16),
     ]
-    if halo:
-        out_shape += [
-            jax.ShapeDtypeStruct((2, kernel_size, TILE_V), jnp.bfloat16),
-            jax.ShapeDtypeStruct((TILE_U, 2 * kernel_size), jnp.bfloat16),
-            jax.ShapeDtypeStruct((kernel_size, 2 * kernel_size), jnp.bfloat16),
-        ]
+    if first_part:
+        out_shape.append(pltpu.VMEM((TILE_U + kernel_size, 2 * kernel_size), jnp.bfloat16))
     out = pl.pallas_call(
         functools.partial(
             grid_body,
             part=part,
             first_part=first_part,
-            halo=halo,
             layout=layout,
             row_slots=row_slots,
             col_slots=col_slots,
@@ -475,11 +495,11 @@
         ],
         compiler_params=pltpu.CompilerParams(vmem_limit_bytes=12 * 2**20),
         name="grid_part",
-    )(plan, in_vmem(kernels), in_hbm(left), in_hbm(right), *carried)
+    )(in_smem(plan), in_vmem(kernels), in_hbm(left), in_hbm(right), *carried)
     return out[:4], out[4:]
 
 
-def merge_body(sums, row_ref, col_ref, corner_ref, out_ref):
+def merge_body(sums, row_ref, col_ref, out_ref):
     kernel_size = row_ref.shape[1]
     patch = sums.shape[1]
     row_slots = out_ref.shape[1] // kernel_size
@@ -489,8 +509,6 @@
     for a in range(row_slots):
         rows = slice(a * kernel_size, (a + 1) * kernel_size)
         edge = col_ref[rows, :].astype(jnp.float32)
-        if a == 0:
-            edge = edge + corner_ref[...].astype(jnp.float32)
         for plane in range(2):
             behind = edge if plane == 0 else pltpu.roll(edge, kernel_size, 1)
             for tile in range(col_slots // 2):
@@ -503,16 +521,16 @@
                 behind = odd
 
 
-def merge_tile(sums, row, col, corner):
+def merge_tile(sums, row, col):
     vmem = pl.BlockSpec(memory_space=pltpu.VMEM)
     return pl.pallas_call(
         merge_body,
-        in_specs=[vmem] * 4,
+        in_specs=[vmem] * 3,
         out_specs=vmem,
         out_shape=jax.ShapeDtypeStruct((2, TILE_U, TILE_V), jnp.float32),
         compiler_params=pltpu.CompilerParams(vmem_limit_bytes=8 * 2**20),
         name="merge_tile",
-    )(in_vmem(sums), row, col, corner)
+    )(*map(in_vmem, (sums, row, col)))
 
 
 def shards(
@@ -538,16 +556,13 @@
     received = arrived.reshape((-1,) + arrived.shape[2:])
     layout = Layout(block_pos.shape[0], (TILE_U // kernel_size) * (TILE_V // kernel_size))
     plan, left, right = plan_blocks(block_pos, block_slot, block_count, vis_left, vis_right, layout)
-    carried, (row, col, corner) = grid_part(plan, 0, received, left, right, None, True, layout)
+    carried, (col,) = grid_part(plan, 0, received, left, right, None, layout)
+    col = from_behind(col, "tv", 1)
+    carried, _ = grid_part(plan, 1, received, left, right, carried, layout)
+    sums, row = row_halo(carried[0], col, kernel_size)
     row = from_behind(row, "tu", 1)
-    col = from_behind(col, "tv", 1)
-    rows, cols = lax.axis_size("tu"), lax.axis_size("tv")
-    diagonal = [
-        (i * cols + j, (i + 1) * cols + j + 1) for i in range(rows - 1) for j in range(cols - 1)
-    ]
-    corner = lax.ppermute(corner, both, diagonal)
-    carried, _ = grid_part(plan, 1, received, left, right, carried, False, layout)
-    return merge_tile(carried[0], row, col, corner)
+    carried, _ = grid_part(plan, 2, received, left, right, [sums, *carried[1:]], layout)
+    return merge_tile(carried[0], row, col)
 
 
 def solution(mesh):

time: 66.4 us -> 63.1 us (0.950)
  the two profiles are of different devices: /device:TPU:9 before, /device:TPU:0 now
where the time goes in v5:
time: 63.1 us; the launch traced here: 62 us
  Pallas kernels  46.5 us (74%)
  starting transfers between devices  10.4 us (16%)
  waiting for transfers between devices  4.23 us (7%)
  between operations  0.75 us (1%)
    pallas_call x1, Pallas kernels, plan_blocks(): pl.pallas_call(functools.partial(plan_body, layout=layout, row_slots=row_...  21.3 us
    pallas_call x3, Pallas kernels, grid_part(): pl.pallas_call(functools.partial(grid_body, part=part, first_part=first_p...  15 us
    pallas_call x1, Pallas kernels, make_kernels(): pl.pallas_call(kernels_body, in_specs=[hbm] * 5, out_specs=pl.BlockSpec(m...  8.73 us
    all_to_all x1, starting transfers between devices, shards(): lax.all_to_all(outgoing, both, split_axis=0, concat_axis=0, tiled=True)  7.3 us
    all_to_all x1, waiting for transfers between devices, shards(): lax.all_to_all(outgoing, both, split_axis=0, concat_axis=0, tiled=True)  4.22 us
    ppermute x2, starting transfers between devices, from_behind(): return lax.ppermute(block, axis, route)  3.13 us
    pallas_call x1, Pallas kernels, merge_tile(): pl.pallas_call(merge_body, in_specs=[vmem] * 3, out_specs=vmem, out_shape...  1.33 us
  transfers between devices with their start and end apart: 3, of which 1 were waited for; matrix products, arithmetic and copies ran while one was open for 0% of the time, Pallas kernels for 50%

profile of v5, /device:TPU:0, one launch (start us, length us, event | category | flops | bytes accessed | tf_op | source)
XLA Modules:
  0.0 62.0 jit_solution(18262828970996281562)
XLA Ops:
  0.0 0.0 copy-start
  0.0 0.0 copy-start.1
  0.0 8.7 %make_kernels.1 = bf16[64,64,128]{2,1,0:T(8,128)(2,1)} custom-call(s32[2,32]{1,0:T(2,128)} %bitcast.8, s32[1,32]{1,0:T(1,128)} %count_hbm.1, f32[4]{0:T(128)} %depth_hbm.1, bf16[4,512,512]{2,1,0:T(8,128)(2,1)} %amp_hbm.1, bf16[4,512,512]{2,1,0:T(8,128)(2,1)} %phase_hbm.1), custom_call_target="tpu_custom_call" | custom-call | tf_op jit(solution)/shard_map/make_kernels/pallas_call | solution.py:146
  8.7 7.3 %all-to-all-start = ((bf16[32,2,64,128]{3,2,1,0:T(8,128)(2,1)}), bf16[32,2,64,128]{3,2,1,0:T(8,128)(2,1)S(1)}, u32[]{:S(2)}, u32[]{:S(2)}) async-start(bf16[32,2,64,128]{3,2,1,0:T(8,128)(2,1)} %bitcast.2), calls=%async_computation | async-start | bytes 2097152 | tf_op jit(solution)/shard_map/all_to_all | solution.py:555
  16.7 0.0 copy-done
  16.7 0.0 copy-done.1
  16.7 21.3 %plan_blocks.1 = (s32[740]{0:T(1024)S(4)}, bf16[576,128,128]{2,1,0:T(8,128)(2,1)}, bf16[576,64,128]{2,1,0:T(8,128)(2,1)}) custom-call(s32[384]{0:T(512)S(1)} %copy-done, s32[384]{0:T(512)S(1)} %copy-done.1, s32[1]{0:T(128)S(6)} %copy.29.count_ref, bf16[384,128,128]{2,1,0:T(8,128)(2,1)} %left_hbm.1, bf16[384,64,128]{2,1,0:T(8,128)(2,1)} %right_hbm.1), custom_call_target="tpu_custom_call" | custom-call | tf_op jit(solution)/shard_map/plan_blocks/pallas_call | solution.py:292
  38.1 4.2 %all-to-all-done = bf16[32,2,64,128]{3,2,1,0:T(8,128)(2,1)S(1)} async-done(((bf16[32,2,64,128]{3,2,1,0:T(8,128)(2,1)}), bf16[32,2,64,128]{3,2,1,0:T(8,128)(2,1)S(1)}, u32[]{:S(2)}, u32[]{:S(2)}) %all-to-all-start) | async-done | bytes 1048608 | tf_op jit(solution)/shard_map/all_to_all | solution.py:555
  42.3 5.1 %grid_part.3 = (f32[32,128,256]{2,1,0:T(8,128)S(1)}, bf16[4,32,128,128]{3,2,1,0:T(8,128)(2,1)S(1)}, bf16[4,32,64,128]{3,2,1,0:T(8,128)(2,1)S(1)}, bf16[4,512,256]{2,1,0:T(8,128)(2,1)S(1)}, bf16[320,128]{1,0:T(8,128)(2,1)S(1)}) custom-call(s32[740]{0:T(1024)S(4)} %get-tuple-element.20.plan_ref, bf16[64,64,128]{2,1,0:T(8,128)(2,1)S(1)} %bitcast.5, ...), custom_call_target="tpu_custom_call" | custom-call | tf_op jit(solution)/shard_map/grid_part/pallas_call | solution.py:479
  47.4 1.3 %collective-permute-start = (bf16[320,128]{1,0:T(8,128)(2,1)S(1)}, bf16[320,128]{1,0:T(8,128)(2,1)S(1)}, u32[]{:S(2)}, u32[]{:S(2)}) collective-permute-start(bf16[320,128]{1,0:T(8,128)(2,1)S(1)} %get-tuple-element.28), channel_id=1, source_target_pairs={{0,1},{1,2},{2,3},{4,5},{5,6},{6,7},{8,9},{9,10},{10,11},{12,13},{... | collective-permute-start | bytes 245768 | tf_op jit(solution)/shard_map/ppermute | solution.py:45
  48.7 3.1 %grid_part.4 = (f32[32,128,256]{2,1,0:T(8,128)S(1)}, bf16[4,32,128,128]{3,2,1,0:T(8,128)(2,1)S(1)}, bf16[4,32,64,128]{3,2,1,0:T(8,128)(2,1)S(1)}, bf16[4,512,256]{2,1,0:T(8,128)(2,1)S(1)}) custom-call(s32[740]{0:T(1024)S(4)} %get-tuple-element.20.plan_ref, ...), custom_call_target="tpu_custom_call", output_to_operand_aliasing={{0}: (4, {}), {1}: (5, {}), {2}: (6, {}), {3}: (7, {})} | custom-call | tf_op jit(solution)/shard_map/grid_part/pallas_call | solution.py:479
  51.7 0.0 collective-permute-done.col_ref
  51.8 0.1 row_halo.1
  51.9 1.8 %collective-permute-start.1 = (bf16[2,64,512]{2,1,0:T(8,128)(2,1)S(1)}, bf16[2,64,512]{2,1,0:T(8,128)(2,1)S(1)}, u32[]{:S(2)}, u32[]{:S(2)}) collective-permute-start(bf16[2,64,512]{2,1,0:T(8,128)(2,1)S(1)} %get-tuple-element.34), channel_id=1, source_target_pairs={{0,4},{4,8},{8,12},{12,16},{16,20},{20,24},{24,28},{1,5},{5,9},{9,... | collective-permute-start | bytes 393224 | tf_op jit(solution)/shard_map/ppermute | solution.py:45
  53.7 6.9 %grid_part.5 = (f32[32,128,256]{2,1,0:T(8,128)S(1)}, bf16[4,32,128,128]{3,2,1,0:T(8,128)(2,1)S(1)}, bf16[4,32,64,128]{3,2,1,0:T(8,128)(2,1)S(1)}, bf16[4,512,256]{2,1,0:T(8,128)(2,1)S(1)}) custom-call(s32[740]{0:T(1024)S(4)} %get-tuple-element.20.plan_ref, ...), custom_call_target="tpu_custom_call", output_to_operand_aliasing={{0}: (4, {}), {1}: (5, {}), {2}: (6, {}), {3}: (7, {})} | custom-call | tf_op jit(solution)/shard_map/grid_part/pallas_call | solution.py:479
  60.6 0.0 collective-permute-done.1.row_ref
  60.6 1.3 %merge_tile.1 = f32[2,256,512]{2,1,0:T(8,128)} custom-call(f32[32,128,256]{2,1,0:T(8,128)S(1)} %get-tuple-element.33.sums, bf16[2,64,512]{2,1,0:T(8,128)(2,1)S(1)} %collective-permute-done.1.row_ref, bf16[320,128]{1,0:T(8,128)(2,1)S(1)} %collective-permute-done.col_ref), custom_call_target="tpu_custom_call" | custom-call | tf_op jit(solution)/shard_map/merge_tile/pallas_call | solution.py:526
Async XLA Ops:
  0.0 16.7 %copy-start = (s32[384]{0:T(512)S(1)}, s32[384]{0:T(512)}, u32[]{:S(2)}) copy-start(s32[384]{0:T(512)} %pos_ref.1) | copy-start | bytes 4612
  0.0 16.7 %copy-start.1 = (s32[384]{0:T(512)S(1)}, s32[384]{0:T(512)}, u32[]{:S(2)}) copy-start(s32[384]{0:T(512)} %slot_ref.1) | copy-start | bytes 4612
  8.7 33.5 %all-to-all-start = ((bf16[32,2,64,128]{3,2,1,0:T(8,128)(2,1)}), bf16[32,2,64,128]{3,2,1,0:T(8,128)(2,1)S(1)}, u32[]{:S(2)}, u32[]{:S(2)}) async-start(bf16[32,2,64,128]{3,2,1,0:T(8,128)(2,1)} %bitcast.2), calls=%async_computation | async-start | bytes 2097152 | tf_op jit(solution)/shard_map/all_to_all | solution.py:555
  47.4 4.4 %collective-permute-start = (bf16[320,128]{1,0:T(8,128)(2,1)S(1)}, bf16[320,128]{1,0:T(8,128)(2,1)S(1)}, u32[]{:S(2)}, u32[]{:S(2)}) collective-permute-start(bf16[320,128]{1,0:T(8,128)(2,1)S(1)} %get-tuple-element.28), channel_id=1, source_target_pairs={{0,1},{1,2},{2,3},{4,5},{5,6},{6,7},{8,9},{9,10},{10,11},{12,13},{... | collective-permute-start | bytes 245768 | tf_op jit(solution)/shard_map/ppermute | solution.py:45
  51.9 8.7 %collective-permute-start.1 = (bf16[2,64,512]{2,1,0:T(8,128)(2,1)S(1)}, bf16[2,64,512]{2,1,0:T(8,128)(2,1)S(1)}, u32[]{:S(2)}, u32[]{:S(2)}) collective-permute-start(bf16[2,64,512]{2,1,0:T(8,128)(2,1)S(1)} %get-tuple-element.34), channel_id=1, source_target_pairs={{0,4},{4,8},{8,12},{12,16},{16,20},{20,24},{24,28},{1,5},{5,9},{9,... | collective-permute-start | bytes 393224 | tf_op jit(solution)/shard_map/ppermute | solution.py:45
